TPU v7x, 32 devices: a whole 2x2x4 slice. The times are simulated.
32 devices in a mesh: bucket: 4 (over y, x), seq: 8 (over z, core).
Axes of the slice: x: 2, y: 2, z: 4, core: 2. Of those that a mesh axis runs over, the one named last changes fastest.
Arguments:
- inputs: bfloat16 [8, 8192, 1024], P('bucket', 'seq'), may hold values from -6 to 6
- cotangent: bfloat16 [8, 8192, 1024], P('bucket', 'seq'), may hold values from -6 to 6
- lengths: int32 [8], P('bucket'), may hold values from 4097 to 8192, as said below
- norm_gains: float32 [2, 1024], replicated, may hold values from 0.5 to 1.5
- norm_biases: float32 [2, 1024], replicated, may hold values from -3 to 3
- in_weight: bfloat16 [1024, 3072], replicated, may hold values from -0.1875 to 0.1875
- in_bias: float32 [3072], replicated, may hold values from -2 to 2
- short_conv: float32 [4, 3072], replicated, may hold values from -3 to 3
- long_skip: float32 [1024], replicated, may hold values from -4 to 4
- filter_in: float32 [33, 64], replicated, may hold values from -1 to 1
- filter_mid: float32 [64, 64], replicated, may hold values from -0.75 to 0.75
- filter_vecs: float32 [4, 64], replicated, may hold values from 0.5 to 2
- filter_out: float32 [64, 1024], replicated, may hold values from -0.01171875 to 0.01171875
- decay: float32 [1024], replicated, may hold values from 0 to 1, as said below
- out_weight: bfloat16 [1024, 1024], replicated, may hold values from -0.1875 to 0.1875
- out_bias: float32 [1024], replicated, may hold values from -2 to 2
- up_weight: bfloat16 [1024, 4096], replicated, may hold values from -0.1875 to 0.1875
- up_bias: float32 [4096], replicated, may hold values from -2 to 2
- down_weight: bfloat16 [4096, 1024], replicated, may hold values from -0.09375 to 0.09375
- down_bias: float32 [1024], replicated, may hold values from -2 to 2
Outputs:
- output: bfloat16 [8, 8192, 1024], P('bucket', 'seq')
- input_grad: float32 [8, 8192, 1024], P('bucket', 'seq')
- grad_norm_gains: float32 [2, 1024], P(None, 'seq')
- grad_norm_biases: float32 [2, 1024], P(None, 'seq')
- grad_in_weight: float32 [1024, 3072], P('seq')
- grad_in_bias: float32 [3072], P('seq')
- grad_short_conv: float32 [4, 3072], P(None, 'seq')
- grad_long_skip: float32 [1024], P('seq')
- grad_filter_in: float32 [33, 64], P(None, 'seq')
- grad_filter_mid: float32 [64, 64], P(None, 'seq')
- grad_filter_vecs: float32 [4, 64], P(None, 'seq')
- grad_filter_out: float32 [64, 1024], P(None, 'seq')
- grad_out_weight: float32 [1024, 1024], P('seq')
- grad_out_bias: float32 [1024], P('seq')
- grad_up_weight: float32 [1024, 4096], P('seq')
- grad_up_bias: float32 [4096], P('seq')
- grad_down_weight: float32 [4096, 1024], P('seq')
- grad_down_bias: float32 [1024], P('seq')
Inputs may be any that keep to these rules, and one draw needn't show every extreme that they name: `lengths`: every sequence belongs to the bucket of 8192 positions: it is longer than 4096; in each group of 2 sequences one has the full 8192 tokens. `decay`: positive rates.
All inputs are finite; a program needn't handle non-finite values.
Results may differ from a plain program's by a relative error of at most 0.017.
Values may be sent and summed in bfloat16 or wider, within the bound.
No kernel may reach another device: no remote copies, remote signals or barrier semaphores. Data moves between devices by JAX's collectives and lax.ppermute only.
A program may use at most 576 MiB of HBM per device.

v0:
```python
import functools
import math

import jax
import jax.numpy as jnp
import ml_dtypes
import numpy as np
from jax import lax
from jax.experimental import pallas as pl
from jax.experimental.pallas import tpu as pltpu
from jax.sharding import PartitionSpec as P

EMB = 33
LEN = 8192
HALF = 64
KB = 128
LANES = 128
STEP_K = 32
STEP_F = 8
ROWS_K = KB + 1
ROWS_F = 2 * KB + 1
MID_TILE = 256
MID_BLOCK = 512

epsilon = 1e-05
f32 = jnp.float32
bf16 = jnp.bfloat16
MIB = 2**20


def lasting(micros):
    return pl.CostEstimate(
        flops=int(micros * 1.1e9), bytes_accessed=1000, transcendentals=0
    )


def passed_along(block, axis, distance):
    devices = range(lax.axis_size(axis))
    route = [(i - distance, i) for i in devices if i - distance in devices]
    return lax.ppermute(block, axis, route)


def best_dot(left, right):
    return jnp.dot(left, right, precision=lax.Precision.HIGHEST)


def dot(left, right):
    return jnp.dot(left, right, preferred_element_type=f32)


def dot_t(left, right):
    return lax.dot_general(left, right, (((1,), (1,)), ((), ())), preferred_element_type=f32)


def positions_embed(length):
    steps = jnp.arange(length, dtype=jnp.int32)
    bands = jnp.arange((EMB - 1) // 2, dtype=jnp.int32)
    angle = 2.0 * math.pi * (steps[:, None] * bands[None, :] % length).astype(f32) / length
    first = steps[:, None].astype(f32) / (length - 1)
    return jnp.concatenate([first, jnp.cos(angle), -jnp.sin(angle)], axis=1)


def filter_taps(filter_in, filter_mid, filter_vecs, columns, rates):
    emb = positions_embed(LEN)
    first = jnp.sin(filter_vecs[1] * (best_dot(emb, filter_in) + filter_vecs[0]))
    second = jnp.sin(filter_vecs[3] * (best_dot(first, filter_mid) + filter_vecs[2]))
    steps = jnp.arange(LEN, dtype=jnp.int32).astype(f32)
    return best_dot(second, columns) * jnp.exp(-rates[None, :] * steps[:, None])


def transform_tables():
    m = np.arange(HALF)
    k = np.arange(KB)
    f = np.arange(HALF)
    turns = ((4 * f[None, :, None] + 1) * (KB * m[None, None, :] + k[:, None, None])) % (4 * LEN)
    phase = 2 * np.pi * turns / (4 * LEN)
    table = np.concatenate([np.cos(phase), -np.sin(phase)], axis=1).astype(np.float32)
    high = table.astype(ml_dtypes.bfloat16)
    low = (table - high.astype(np.float32)).astype(ml_dtypes.bfloat16)
    onward = np.concatenate([high, low], axis=2)
    back = np.ascontiguousarray(np.swapaxes(table, 1, 2)).astype(ml_dtypes.bfloat16)
    angle = 2 * np.pi * ((k[:, None] * k[None]) % KB) / KB
    cos, sin = np.cos(angle), np.sin(angle)
    inner = np.block([[cos, sin], [-sin, cos]])
    return (
        jnp.asarray(onward),
        jnp.asarray(back),
        jnp.asarray(inner.astype(ml_dtypes.bfloat16)),
        jnp.asarray(np.ascontiguousarray(inner.T).astype(ml_dtypes.bfloat16)),
    )


def looped(count, unroll, body):
    def step(i, carry):
        for u in range(unroll):
            body(i * unroll + u)
        return carry

    lax.fori_loop(0, count // unroll, step, 0)


def fetch(src, dst, sems, first, pieces):
    rows = dst.shape[0] // pieces
    copies = []
    for n in range(pieces):
        part = pl.ds(n * rows, rows)
        copy = pltpu.make_async_copy(src.at[part], dst.at[part], sems.at[first + n])
        copy.start()
        copies.append(copy)
    return copies


def outer_stage(first, count, exact, src, table, dst):
    def body(n):
        k = first + n
        rows = src[pl.ds(k, HALF, stride=ROWS_K), :]
        high = rows.astype(bf16)
        out = dot(table[k], jnp.concatenate([high, high], axis=0))
        if not exact:
            low = (rows - high.astype(f32)).astype(bf16)
            out = out + dot(table[k, :, :HALF], low)
        dst[pl.ds(k, HALF, stride=ROWS_F), :] = out[:HALF]
        dst[pl.ds(k + KB, HALF, stride=ROWS_F), :] = out[HALF:]

    looped(count, STEP_K, body)


def outer_back(first, count, src, table, dst):
    def body(n):
        k = first + n
        real = src[pl.ds(k, HALF, stride=ROWS_F), :]
        imag = src[pl.ds(k + KB, HALF, stride=ROWS_F), :]
        rows = jnp.concatenate([real, imag], axis=0).astype(bf16)
        dst[pl.ds(k, HALF, stride=ROWS_K), :] = dot(table[k], rows)

    looped(count, STEP_K, body)


def spaced(src, dst, first, count):
    for m in range(first, first + count):
        dst[m * ROWS_K : m * ROWS_K + KB] = src[m * KB : (m + 1) * KB].astype(f32)


def packed(src, dst):
    for m in range(HALF):
        rows = src[m * ROWS_K : m * ROWS_K + KB] * (1.0 / LEN)
        dst[m * KB : (m + 1) * KB] = rows.astype(dst.dtype)


def row_pair(at):
    row = at * (2 * ROWS_F)
    return pl.ds(row, 2 * KB), pl.ds(row + ROWS_F, 2 * KB)


PIECES = 4


def conv_kernel(backward, x_ref, h_ref, *refs):
    if backward:
        spec_in, *refs = refs
    ta_ref, tai_ref, tb, tbi = refs[:4]
    y_ref, spec_ref, token, x, h, spec, ta, tai, xs, mid, sems = refs[-11:]
    token[...] = jnp.zeros_like(token)
    x_in = fetch(x_ref, x, sems, 0, 2)
    ta_in = fetch(ta_ref, ta, sems, 2, PIECES)
    h_in = fetch(h_ref, h, sems, 2 + PIECES, PIECES)
    s_in = fetch(spec_in, spec, sems, 2 + 2 * PIECES, PIECES) if backward else ()
    tai_in = fetch(tai_ref, tai, sems, 2 + 3 * PIECES, 1)
    half = HALF // 2
    for n in range(2):
        x_in[n].wait()
        spaced(x, xs, n * half, half)
    for n in range(PIECES):
        ta_in[n].wait()
        outer_stage(n * KB // PIECES, KB // PIECES, True, xs, ta, mid)

    def inner(first):
        def body(n):
            at = first + n
            left, right = row_pair(at)
            both = jnp.concatenate([mid[left, :].astype(bf16), mid[right, :].astype(bf16)], axis=1)
            freq = dot(tb[...], both)
            prods = []
            for v in range(2):
                f = 2 * at + v
                re = freq[:KB, v * LANES : (v + 1) * LANES]
                im = freq[KB:, v * LANES : (v + 1) * LANES]
                hr = h[f, :KB].astype(f32)
                hi = h[f, KB:].astype(f32)
                if backward:
                    pr, pi = re * hr + im * hi, im * hr - re * hi
                    sr = spec[f, :KB].astype(f32)
                    si = spec[f, KB:].astype(f32)
                    spec[f, :KB] = (re * sr + im * si).astype(bf16)
                    spec[f, KB:] = (im * sr - re * si).astype(bf16)
                else:
                    pr, pi = re * hr - im * hi, re * hi + im * hr
                    spec[f, :KB] = re.astype(bf16)
                    spec[f, KB:] = im.astype(bf16)
                prods.append(jnp.concatenate([pr, pi], axis=0).astype(bf16))
            out = dot(tbi[...], jnp.concatenate(prods, axis=1))
            mid[left, :] = out[:, :LANES]
            mid[right, :] = out[:, LANES:]

        return body

    leaving = []
    rows = HALF // PIECES
    for n in range(PIECES):
        h_in[n].wait()
        if backward:
            s_in[n].wait()
        looped(rows // 2, STEP_F, inner(n * rows // 2))
        part = pl.ds(n * rows, rows)
        copy = pltpu.make_async_copy(spec.at[part], spec_ref.at[part], sems.at[3 + 3 * PIECES + n])
        copy.start()
        leaving.append(copy)
    tai_in[0].wait()
    outer_back(0, KB, mid, tai, xs)
    packed(xs, y_ref)
    for copy in leaving:
        copy.wait()


def whole_spec(shape):
    return pl.BlockSpec(shape, lambda i: (0,) * len(shape))


def once(shape):
    return pl.BlockSpec(shape, lambda i: (0,) * len(shape), pipeline_mode=pl.Buffered(1))


TOKEN = jax.ShapeDtypeStruct((8, LANES), f32)
ANYWHERE = pl.BlockSpec(memory_space=pl.ANY)
IN_VMEM = pl.BlockSpec(memory_space=pltpu.VMEM)
SPECTRUM = (HALF, 2 * KB, LANES)


def long_conv(rows, taps_spec, tables, data_spec=None, after=()):
    backward = data_spec is not None
    onward, back, inner, inner_back = tables
    extra = [data_spec] if backward else []
    return pl.pallas_call(
        functools.partial(conv_kernel, backward),
        in_specs=[ANYWHERE] * (4 + len(extra)) + [IN_VMEM] * 2 + [ANYWHERE] * len(after),
        out_specs=[IN_VMEM, ANYWHERE, IN_VMEM],
        out_shape=[
            jax.ShapeDtypeStruct((LEN, LANES), bf16),
            jax.ShapeDtypeStruct(SPECTRUM, bf16),
            TOKEN,
        ],
        scratch_shapes=[
            pltpu.VMEM((LEN, LANES), bf16),
            pltpu.VMEM(SPECTRUM, bf16),
            pltpu.VMEM(SPECTRUM, bf16),
            pltpu.VMEM(onward.shape, bf16),
            pltpu.VMEM(back.shape, bf16),
            pltpu.VMEM((HALF * ROWS_K, LANES), f32),
            pltpu.VMEM((HALF * ROWS_F, LANES), f32),
            pltpu.SemaphoreType.DMA((3 + 4 * PIECES,)),
        ],
        compiler_params=pltpu.CompilerParams(vmem_limit_bytes=60 * MIB),
        cost_estimate=lasting(14),
    )(rows, taps_spec, *extra, onward, back, inner, inner_back, *after)


def taps_kernel(x_ref, ta_ref, tb, *refs):
    h_ref, x, ta, xs, mid, h, sems = refs[-7:]
    x_in = fetch(x_ref, x, sems, 0, 2)
    ta_in = fetch(ta_ref, ta, sems, 2, PIECES)
    half = HALF // 2
    for n in range(2):
        x_in[n].wait()
        spaced(x, xs, n * half, half)
    for n in range(PIECES):
        ta_in[n].wait()
        outer_stage(n * KB // PIECES, KB // PIECES, False, xs, ta, mid)

    def body(at):
        left, right = row_pair(at)
        both = jnp.concatenate([mid[left, :].astype(bf16), mid[right, :].astype(bf16)], axis=1)
        freq = dot(tb[...], both)
        h[2 * at] = freq[:, :LANES].astype(bf16)
        h[2 * at + 1] = freq[:, LANES:].astype(bf16)

    leaving = []
    rows = HALF // PIECES
    for n in range(PIECES):
        looped(rows // 2, STEP_F, lambda at, n=n: body(n * rows // 2 + at))
        part = pl.ds(n * rows, rows)
        copy = pltpu.make_async_copy(h.at[part], h_ref.at[part], sems.at[2 + PIECES + n])
        copy.start()
        leaving.append(copy)
    for copy in leaving:
        copy.wait()


def taps_transform(taps, tables, after):
    onward, _, inner, _ = tables
    return pl.pallas_call(
        taps_kernel,
        in_specs=[ANYWHERE, ANYWHERE, IN_VMEM] + [ANYWHERE] * len(after),
        out_specs=ANYWHERE,
        out_shape=jax.ShapeDtypeStruct(SPECTRUM, bf16),
        scratch_shapes=[
            pltpu.VMEM((LEN, LANES), f32),
            pltpu.VMEM(onward.shape, bf16),
            pltpu.VMEM((HALF * ROWS_K, LANES), f32),
            pltpu.VMEM((HALF * ROWS_F, LANES), f32),
            pltpu.VMEM(SPECTRUM, bf16),
            pltpu.SemaphoreType.DMA((2 + 2 * PIECES,)),
        ],
        compiler_params=pltpu.CompilerParams(vmem_limit_bytes=60 * MIB),
        cost_estimate=lasting(15),
    )(taps, onward, inner, *after)


def taps_back_kernel(count, *refs):
    specs = refs[:count]
    tai_ref, tbi = refs[count : count + 2]
    y_ref, token, tai, mid, ys, held, sems = refs[-7:]
    token[...] = jnp.zeros_like(token)
    tai_in = fetch(tai_ref, tai, sems, 0, 1)
    arrivals = [
        fetch(specs[c], held.at[c], sems, 1 + c * PIECES, PIECES) for c in range(count)
    ]

    def body(at):
        left, right = row_pair(at)
        prods = []
        for v in range(2):
            total = held[0, 2 * at + v].astype(f32)
            for c in range(1, count):
                total = total + held[c, 2 * at + v].astype(f32)
            prods.append(total.astype(bf16))
        out = dot(tbi[...], jnp.concatenate(prods, axis=1))
        mid[left, :] = out[:, :LANES]
        mid[right, :] = out[:, LANES:]

    rows = HALF // PIECES
    for n in range(PIECES):
        for c in range(count):
            arrivals[c][n].wait()
        looped(rows // 2, STEP_F, lambda at, n=n: body(n * rows // 2 + at))
    tai_in[0].wait()
    outer_back(0, KB, mid, tai, ys)
    packed(ys, y_ref)


def taps_back(specs, tables, after):
    _, back, _, inner_back = tables
    count = len(specs)
    return pl.pallas_call(
        functools.partial(taps_back_kernel, count),
        in_specs=[ANYWHERE] * (count + 1) + [IN_VMEM] + [ANYWHERE] * len(after),
        out_specs=[IN_VMEM, IN_VMEM],
        out_shape=[jax.ShapeDtypeStruct((LEN, LANES), f32), TOKEN],
        scratch_shapes=[
            pltpu.VMEM(back.shape, bf16),
            pltpu.VMEM((HALF * ROWS_F, LANES), f32),
            pltpu.VMEM((HALF * ROWS_K, LANES), f32),
            pltpu.VMEM((count,) + SPECTRUM, bf16),
            pltpu.SemaphoreType.DMA((1 + count * PIECES,)),
        ],
        compiler_params=pltpu.CompilerParams(vmem_limit_bytes=60 * MIB),
        cost_estimate=lasting(15),
    )(*specs, back, inner_back, *after)


def normalized(rows):
    mean = jnp.mean(rows, axis=-1, keepdims=True)
    centered = rows - mean
    spread = jnp.mean(centered * centered, axis=-1, keepdims=True)
    root = lax.rsqrt(spread + epsilon)
    return centered * root, root


def norm_back(grad, gain, xhat, root):
    g = grad * gain
    mean = jnp.mean(g, axis=-1, keepdims=True)
    along = jnp.mean(g * xhat, axis=-1, keepdims=True)
    return (g - mean - xhat * along) * root


def column_sum(block):
    return jnp.sum(block, axis=0, keepdims=True)


def joined(ref):
    if ref.shape[0] == 1:
        return ref[0]
    return jnp.concatenate([ref[b] for b in range(ref.shape[0])], axis=1)


def spread_out(ref, first, block):
    chans = ref.shape[2]
    width = block.shape[1]
    if chans >= first + width and ref.shape[0] == 1:
        ref[0, :, first : first + width] = block
        return
    for at in range(0, width, chans):
        ref[(first + at) // chans] = block[:, at : at + chans]


def front_kernel(
    x_ref, rim_ref, flag_ref, gain, shift, w_ref, b_ref, short, *refs
):
    normed_ref, proj_ref, mixed_ref, carried_ref, token, tail = refs[-6:]
    i = pl.program_id(0)
    tile, dim = x_ref.shape
    token[...] = jnp.zeros_like(token)

    @pl.when(i == 0)
    def _():
        rows, _ = normalized(rim_ref[...].astype(f32))
        rows = (rows * gain[...] + shift[...]).astype(bf16)
        edge = (dot(rows, w_ref[...]) + b_ref[...]).astype(bf16).astype(f32)
        tail[...] = edge[8:] * flag_ref[...]

    xhat, _ = normalized(x_ref[...].astype(f32))
    normed = (xhat * gain[...] + shift[...]).astype(bf16)
    normed_ref[...] = normed
    block = 256
    at_row = lax.broadcasted_iota(jnp.int32, (tile, block), 0)
    for first in range(0, dim, block):
        parts = []
        for stream in range(3):
            cols = slice(stream * dim + first, stream * dim + first + block)
            proj = (dot(normed, w_ref[:, cols]) + b_ref[:, cols]).astype(bf16)
            proj_ref[:, cols] = proj
            proj = proj.astype(f32)
            one = jnp.where(at_row == 0, tail[7:8, cols], pltpu.roll(proj, 1, 0))
            two = jnp.where(
                at_row == 0,
                tail[6:7, cols],
                jnp.where(at_row == 1, tail[7:8, cols], pltpu.roll(proj, 2, 0)),
            )
            mixed = (
                short[0:1, cols] * two
                + short[1:2, cols] * one
                + short[2:3, cols] * proj
                + short[3:4, cols]
            )
            mixed_ref[:, cols] = mixed.astype(bf16)
            tail[:, cols] = proj[tile - 8 :]
            parts.append(mixed)
        spread_out(carried_ref, first, (parts[1] * parts[2]).astype(bf16))


def front(s, inputs, rims, flag, gain, shift, weight, bias, short, blocks, shared):
    seqs, width, dim = inputs.shape
    tile = min(256, width)
    tiles = width // tile
    wide = weight.shape[1]
    tok = seqs * width
    stacked = lambda cols: pl.BlockSpec((tile, cols), lambda i: (s * tiles + i, 0))
    operands = (inputs, rims, flag, gain, shift, weight, bias, short)
    return pl.pallas_call(
        front_kernel,
        grid=(tiles,),
        in_specs=[
            pl.BlockSpec((None, tile, dim), lambda i: (s, i, 0)),
            pl.BlockSpec((None,) + rims.shape[1:], lambda i: (s, 0, 0)),
            once((1, 1)),
            once((1, dim)),
            once((1, dim)),
            once((dim, wide)),
            once((1, wide)),
            once((4, wide)),
        ]
        + [ANYWHERE] * len(shared),
        out_specs=[
            stacked(dim),
            stacked(wide),
            stacked(wide),
            pl.BlockSpec((blocks, tile, dim // blocks), lambda i: (0, i, 0)),
            whole_spec(TOKEN.shape),
        ],
        out_shape=[
            jax.ShapeDtypeStruct((tok, dim), bf16),
            jax.ShapeDtypeStruct((tok, wide), bf16),
            jax.ShapeDtypeStruct((tok, wide), bf16),
            jax.ShapeDtypeStruct((blocks, width, dim // blocks), bf16),
            TOKEN,
        ],
        input_output_aliases={len(operands) + n: n for n in range(len(shared))},
        scratch_shapes=[pltpu.VMEM((8, wide), f32)],
        compiler_params=pltpu.CompilerParams(vmem_limit_bytes=60 * MIB),
        cost_estimate=lasting(20),
    )(*operands, *shared)


def gelu_and_slope(hidden):
    size = jnp.abs(hidden)
    bell = jnp.exp(hidden * hidden * -0.5)
    t = pl.reciprocal(1.0 + size * (0.3275911 / math.sqrt(2.0)), approx=False)
    poly = 0.5 * 1.061405429
    for term in (-1.453152027, 1.421413741, -0.284496736, 0.254829592):
        poly = poly * t + 0.5 * term
    rest = poly * t * bell
    below = jnp.where(hidden >= 0, 1.0 - rest, rest)
    return hidden * below, below + hidden * (bell * (1.0 / math.sqrt(2.0 * math.pi)))


def mid_kernel(
    count_ref, conv_ref, carried_ref, gate_ref, x_ref, cot_ref, skip, gain, shift, w_out, b_out,
    w_up, b_up, w_down, b_down, *refs
):
    (
        out_ref, act_ref, gh_ref, normed_ref, gated_ref, gdi_ref, branch_ref, resid_ref, ggo_ref,
        gconv_ref, d_gain, d_shift, d_down_b, d_up_b, d_out_b, d_skip
    ) = refs[-16:]
    i = pl.program_id(0)
    tile, dim = x_ref.shape
    hid = w_up.shape[1]

    @pl.when(i == 0)
    def _():
        for ref in (d_gain, d_shift, d_down_b, d_up_b, d_out_b, d_skip):
            ref[...] = jnp.zeros_like(ref)

    place = i * tile + lax.broadcasted_iota(jnp.int32, (tile, 1), 0)
    mask = (place < count_ref[0]).astype(f32)
    carried = joined(carried_ref).astype(f32)
    gate = gate_ref[...].astype(f32)
    long_out = joined(conv_ref).astype(f32) + skip[...] * carried
    gated = (gate * long_out).astype(bf16)
    gated_ref[...] = gated
    resid = x_ref[...].astype(f32) + dot(gated, w_out[...]) + b_out[...]
    xhat, root = normalized(resid)
    normed = (xhat * gain[...] + shift[...]).astype(bf16)
    normed_ref[...] = normed
    grad_final = cot_ref[...].astype(f32) * mask
    gdi = grad_final.astype(bf16)
    gdi_ref[...] = gdi
    d_down_b[...] += column_sum(grad_final)
    final = resid + b_down[...]
    back = jnp.zeros((tile, dim), f32)
    block = MID_BLOCK
    for first in range(0, hid, block):
        cols = slice(first, first + block)
        hidden = dot(normed, w_up[:, cols]) + b_up[:, cols]
        grad_act = dot_t(gdi, w_down[cols, :])
        act, slope = gelu_and_slope(hidden)
        act = act.astype(bf16)
        grad_hidden = (slope * grad_act).astype(bf16)
        act_ref[:, cols] = act
        gh_ref[:, cols] = grad_hidden
        d_up_b[:, cols] += column_sum(grad_hidden.astype(f32))
        final = final + dot(act, w_down[cols, :])
        back = back + dot_t(grad_hidden, w_up[:, cols])
    out_ref[...] = (final * mask).astype(bf16)
    d_shift[...] += column_sum(back)
    d_gain[...] += column_sum(back * xhat)
    grad_resid = grad_final + norm_back(back, gain[...], xhat, root)
    resid_ref[...] = grad_resid
    branch = grad_resid.astype(bf16)
    branch_ref[...] = branch
    d_out_b[...] += column_sum(branch.astype(f32))
    grad_gated = dot_t(branch, w_out[...])
    ggo_ref[...] = (grad_gated * long_out).astype(bf16)
    grad_long = grad_gated * gate
    d_skip[...] += column_sum(grad_long * carried)
    spread_out(gconv_ref, 0, grad_long.astype(bf16))


def middle(s, count, conv, carried, mixed, inputs, cot, skip, gain, shift, w_out, b_out, w_up,
           b_up, w_down, b_down, shared, after):
    seqs, width, dim = inputs.shape
    hid = w_up.shape[1]
    blocks, _, chans = carried.shape
    tile = min(MID_TILE, width)
    tiles = width // tile
    split = pl.BlockSpec((blocks, tile, chans), lambda i: (0, i, 0))
    stacked = lambda cols: pl.BlockSpec((tile, cols), lambda i: (i + s * tiles, 0))
    layer = pl.BlockSpec((None, tile, dim), lambda i: (s, i, 0))
    tok = seqs * width
    sums = [dim, dim, dim, hid, dim, dim]
    shapes = [
        ((seqs, width, dim), bf16),
        ((tok, hid), bf16),
        ((tok, hid), bf16),
        ((tok, dim), bf16),
        ((tok, dim), bf16),
        ((tok, dim), bf16),
        ((tok, dim), bf16),
        ((tok, dim), f32),
        ((tok, dim), bf16),
        ((blocks, width, chans), bf16),
    ] + [((1, n), f32) for n in sums]
    operands = (count, conv, carried, mixed, inputs, cot, skip, gain, shift, w_out, b_out, w_up,
                b_up, w_down, b_down)
    aliases = {len(operands) + n: n for n in range(len(shared))}
    return pl.pallas_call(
        mid_kernel,
        grid=(tiles,),
        in_specs=[
            pl.BlockSpec(memory_space=pltpu.SMEM),
            split,
            split,
            stacked(dim),
            layer,
            layer,
            once((1, dim)),
            once((1, dim)),
            once((1, dim)),
            once((dim, dim)),
            once((1, dim)),
            once((dim, hid)),
            once((1, hid)),
            once((hid, dim)),
            once((1, dim)),
        ]
        + [ANYWHERE] * (len(shared) + len(after)),
        out_specs=[
            layer,
            stacked(hid),
            stacked(hid),
            stacked(dim),
            stacked(dim),
            stacked(dim),
            stacked(dim),
            stacked(dim),
            stacked(dim),
            split,
        ]
        + [whole_spec((1, n)) for n in sums],
        out_shape=[jax.ShapeDtypeStruct(shape, kind) for shape, kind in shapes],
        input_output_aliases=aliases,
        compiler_params=pltpu.CompilerParams(vmem_limit_bytes=60 * MIB),
        cost_estimate=lasting(66),
    )(*operands, *shared, *after)


def grad_rows(now, proj, cols, head, short, out, d_short, d_bias):
    tile, block = now.shape
    at_row = lax.broadcasted_iota(jnp.int32, (tile, block), 0)
    one = jnp.where(at_row == tile - 1, head[0:1, cols], pltpu.roll(now, tile - 1, 0))
    two = jnp.where(
        at_row == tile - 1,
        head[1:2, cols],
        jnp.where(at_row == tile - 2, head[0:1, cols], pltpu.roll(now, tile - 2, 0)),
    )
    head[:, cols] = now[:8]
    proj = proj.astype(f32)
    d_short[0:1, cols] += column_sum(two * proj)
    d_short[1:2, cols] += column_sum(one * proj)
    d_short[2:3, cols] += column_sum(now * proj)
    d_short[3:4, cols] += column_sum(now)
    grad = short[2:3, cols] * now + short[1:2, cols] * one + short[0:1, cols] * two
    grad = grad.astype(bf16)
    out[:, cols] = grad
    d_bias[:, cols] += column_sum(grad.astype(f32))


def gate_kernel(tiles, ggo_ref, proj_ref, rim_ref, short, *refs):
    out, d_short, d_bias, token, head = refs[-5:]
    i = pl.program_id(0)
    dim = ggo_ref.shape[1]
    token[...] = jnp.zeros_like(token)

    @pl.when(i == 0)
    def _():
        d_short[...] = jnp.zeros_like(d_short)
        d_bias[...] = jnp.zeros_like(d_bias)

    @pl.when(i % tiles == 0)
    def _():
        head[...] = rim_ref[...]

    block = 256
    for first in range(0, dim, block):
        cols = slice(first, first + block)
        grad_rows(ggo_ref[:, cols].astype(f32), proj_ref[:, cols], cols, head, short, out, d_short,
                  d_bias)


def gate_grads(seqs, ggo, proj, rims, short, after):
    tok, dim = ggo.shape
    width = tok // seqs
    tile = min(256, width)
    tiles = width // tile
    by_row = pl.BlockSpec(
        (tile, dim), lambda i: ((i // tiles) * tiles + tiles - 1 - i % tiles, 0)
    )
    return pl.pallas_call(
        functools.partial(gate_kernel, tiles),
        grid=(seqs * tiles,),
        in_specs=[
            by_row,
            by_row,
            pl.BlockSpec((None, 8, dim), lambda i: (i // tiles, 0, 0)),
            once((4, dim)),
        ]
        + [ANYWHERE] * len(after),
        out_specs=[by_row, whole_spec((4, dim)), whole_spec((1, dim)), whole_spec(TOKEN.shape)],
        out_shape=[
            jax.ShapeDtypeStruct((tok, dim), bf16),
            jax.ShapeDtypeStruct((4, dim), f32),
            jax.ShapeDtypeStruct((1, dim), f32),
            TOKEN,
        ],
        scratch_shapes=[pltpu.VMEM((8, dim), f32)],
        compiler_params=pltpu.CompilerParams(vmem_limit_bytes=60 * MIB),
        cost_estimate=lasting(7),
    )(ggo, proj, rims, short, *after)


def pair_kernel(gback_ref, gconv_ref, gates_ref, proj_ref, rim_ref, skip, short, *refs):
    out, d_short, d_bias, token, head = refs[-5:]
    i = pl.program_id(0)
    wide = rim_ref.shape[1]
    dim = wide // 2
    token[...] = jnp.zeros_like(token)

    @pl.when(i == 0)
    def _():
        head[...] = rim_ref[...]
        d_short[...] = jnp.zeros_like(d_short)
        d_bias[...] = jnp.zeros_like(d_bias)

    grad_carried = joined(gback_ref).astype(f32) + skip[...] * joined(gconv_ref).astype(f32)
    block = 256
    for first in range(0, dim, block):
        grad = grad_carried[:, first : first + block]
        for stream in range(2):
            cols = slice(stream * dim + first, stream * dim + first + block)
            other = slice(dim + (1 - stream) * dim + first, dim + (1 - stream) * dim + first + block)
            past = slice(dim + cols.start, dim + cols.stop)
            now = grad * gates_ref[:, other].astype(f32)
            grad_rows(now, proj_ref[:, past], cols, head, short, out, d_short, d_bias)


def pair_grads(s, seqs, gback, gconv, mixed, proj, rim, skip, short, shared, after):
    blocks, width, chans = gback.shape
    wide3 = mixed.shape[1]
    dim = blocks * chans
    wide = 2 * dim
    tile = min(256, width)
    tiles = width // tile
    back_row = lambda cols: pl.BlockSpec((tile, cols), lambda i: (s * tiles + tiles - 1 - i, 0))
    split = pl.BlockSpec((blocks, tile, chans), lambda i: (0, tiles - 1 - i, 0))
    operands = (gback, gconv, mixed, proj, rim, skip, short)
    return pl.pallas_call(
        pair_kernel,
        grid=(tiles,),
        in_specs=[
            split,
            split,
            back_row(wide3),
            back_row(wide3),
            once((8, wide)),
            once((1, dim)),
            once((4, wide)),
        ]
        + [ANYWHERE] * (len(shared) + len(after)),
        out_specs=[
            back_row(wide),
            whole_spec((4, wide)),
            whole_spec((1, wide)),
            whole_spec(TOKEN.shape),
        ],
        out_shape=[
            jax.ShapeDtypeStruct((seqs * width, wide), bf16),
            jax.ShapeDtypeStruct((4, wide), f32),
            jax.ShapeDtypeStruct((1, wide), f32),
            TOKEN,
        ],
        input_output_aliases={len(operands) + n: n for n in range(len(shared))},
        scratch_shapes=[pltpu.VMEM((8, wide), f32)],
        compiler_params=pltpu.CompilerParams(vmem_limit_bytes=60 * MIB),
        cost_estimate=lasting(11),
    )(*operands, *shared, *after)


def input_kernel(first_ref, rest_ref, x_ref, resid_ref, gain, w_ref, *refs):
    igrad_ref, d_gain, d_shift, token = refs[-4:]
    dim = x_ref.shape[1]
    token[...] = jnp.zeros_like(token)

    @pl.when(pl.program_id(0) == 0)
    def _():
        d_gain[...] = jnp.zeros_like(d_gain)
        d_shift[...] = jnp.zeros_like(d_shift)

    grad = dot_t(first_ref[...], w_ref[:, :dim]) + dot_t(rest_ref[...], w_ref[:, dim:])
    xhat, root = normalized(x_ref[...].astype(f32))
    d_shift[...] += column_sum(grad)
    d_gain[...] += column_sum(grad * xhat)
    igrad_ref[...] = resid_ref[...] + norm_back(grad, gain[...], xhat, root)


def input_grads(s, first, rest, inputs, resid, gain, weight, shared, after):
    seqs, width, dim = inputs.shape
    wide = weight.shape[1]
    tile = min(256, width)
    tiles = width // tile
    stacked = lambda cols: pl.BlockSpec((tile, cols), lambda i: (s * tiles + i, 0))
    layer = pl.BlockSpec((None, tile, dim), lambda i: (s, i, 0))
    operands = (first, rest, inputs, resid, gain, weight)
    return pl.pallas_call(
        input_kernel,
        grid=(tiles,),
        in_specs=[
            stacked(dim),
            stacked(wide - dim),
            layer,
            stacked(dim),
            once((1, dim)),
            once((dim, wide)),
        ]
        + [ANYWHERE] * (len(shared) + len(after)),
        out_specs=[layer, whole_spec((1, dim)), whole_spec((1, dim)), whole_spec(TOKEN.shape)],
        out_shape=[
            jax.ShapeDtypeStruct((seqs, width, dim), f32),
            jax.ShapeDtypeStruct((1, dim), f32),
            jax.ShapeDtypeStruct((1, dim), f32),
            TOKEN,
        ],
        input_output_aliases={len(operands) + n: n for n in range(len(shared))},
        compiler_params=pltpu.CompilerParams(vmem_limit_bytes=60 * MIB),
        cost_estimate=lasting(14),
    )(*operands, *shared, *after)


def over_tokens(left, right):
    return lax.dot_general(left, right, (((0,), (0,)), ((), ())), preferred_element_type=f32)


def tall_kernel(left, right, *refs):
    out, token = refs[-2:]
    token[...] = jnp.zeros_like(token)
    total = over_tokens(left[...], right[...])
    rows = out.shape[3]
    for b in range(out.shape[1]):
        out[0, b, 0] = total[b * rows : (b + 1) * rows].astype(bf16)


def flat_kernel(left, right, *refs):
    out, token = refs[-2:]
    token[...] = jnp.zeros_like(token)
    total = over_tokens(left[...], right[...])
    cores, buckets, zs, rows, _ = out.shape
    for z in range(zs):
        for c in range(cores):
            for b in range(buckets):
                at = ((cores * z + c) * buckets + b) * rows
                out[c, b, z] = total[at : at + rows].astype(bf16)


def two_kernel(steps, left, right, left2, right2, *refs):
    i = pl.program_id(0)

    @pl.when(i < steps)
    def _():
        flat_kernel(left, right, *refs)

    @pl.when(i >= steps)
    def _():
        flat_kernel(left2, right2, *refs)


def two_weight_grads(left, right, left2, right2, parts, buckets, after):
    tok, high = left.shape
    cols = right.shape[1]
    rows = high // parts // buckets
    if rows % 32:
        one, _ = weight_grad(left, right, parts, buckets, after)
        two, _ = weight_grad(left2, right2, parts, buckets, after)
        return jnp.concatenate([one, two], axis=1), after[0]
    block = min(512, cols)
    steps = cols // block
    shape = (2, buckets, parts // 2, rows, 2 * cols)
    total, token = pl.pallas_call(
        functools.partial(two_kernel, steps),
        grid=(2 * steps,),
        in_specs=[
            once((tok, high)),
            pl.BlockSpec((tok, block), lambda i: (0, jnp.minimum(i, steps - 1))),
            once((tok, high)),
            pl.BlockSpec((tok, block), lambda i: (0, jnp.maximum(i - steps, 0))),
        ]
        + [ANYWHERE] * len(after),
        out_specs=[
            pl.BlockSpec(shape[:4] + (block,), lambda i: (0, 0, 0, 0, i)),
            whole_spec(TOKEN.shape),
        ],
        out_shape=[jax.ShapeDtypeStruct(shape, bf16), TOKEN],
        compiler_params=pltpu.CompilerParams(vmem_limit_bytes=60 * MIB),
        cost_estimate=lasting(18),
    )(left, right, left2, right2, *after)
    return total.reshape(high, 2 * cols), token


def weight_grad(left, right, parts, buckets, after):
    tok, high = left.shape
    cols = right.shape[1]
    share = high // parts
    rows = share // buckets
    shape = (2, buckets, parts // 2, rows, cols)
    if rows % 32:
        total = jnp.einsum("tk,tn->kn", left, right, preferred_element_type=f32).astype(bf16)
        total = total.reshape(parts // 2, 2, buckets, rows, cols)
        return jnp.transpose(total, (1, 2, 0, 3, 4)).reshape(high, cols), after[0]
    tall = share % 512 == 0
    block = min(512, cols)
    if tall:
        steps = parts
        specs = [pl.BlockSpec((tok, share), lambda i: (0, i)), once((tok, cols))]
        out = pl.BlockSpec((1, buckets, 1, rows, cols), lambda i: (i % 2, 0, i // 2, 0, 0))
    else:
        steps = cols // block
        specs = [once((tok, high)), pl.BlockSpec((tok, block), lambda i: (0, i))]
        out = pl.BlockSpec(shape[:4] + (block,), lambda i: (0, 0, 0, 0, i))
    total, token = pl.pallas_call(
        tall_kernel if tall else flat_kernel,
        grid=(steps,),
        in_specs=specs + [ANYWHERE] * len(after),
        out_specs=[out, whole_spec(TOKEN.shape)],
        out_shape=[jax.ShapeDtypeStruct(shape, bf16), TOKEN],
        compiler_params=pltpu.CompilerParams(vmem_limit_bytes=60 * MIB),
        cost_estimate=lasting(23),
    )(left, right, *after)
    return total.reshape(high, cols), token


def swapped(block, axis, groups=None):
    return lax.all_to_all(
        block, axis, split_axis=0, concat_axis=0, tiled=True, axis_index_groups=groups
    )


def added(block):
    total = block[0].astype(f32)
    for n in range(1, block.shape[0]):
        total = total + block[n].astype(f32)
    return total


def tied(block, token):
    return block + (token[0, 0] * 0.0).astype(block.dtype)


def launch_kernel(*refs):
    refs[-1][...] = jnp.zeros_like(refs[-1])


def launched(block, after):
    return pl.pallas_call(
        launch_kernel,
        in_specs=[ANYWHERE] * (1 + len(after)),
        out_specs=[ANYWHERE, pl.BlockSpec(memory_space=pltpu.VMEM)],
        out_shape=[jax.ShapeDtypeStruct(block.shape, block.dtype), TOKEN],
        input_output_aliases={0: 0},
        cost_estimate=lasting(1),
    )(block, *after)


def pair_groups(parts):
    return [[2 * z, 2 * z + 1] for z in range(parts // 2)]


def pair_sum(block, parts):
    return lax.psum_scatter(
        block, "seq", scatter_dimension=0, tiled=True, axis_index_groups=pair_groups(parts)
    )


def bucket_sum(block):
    return lax.psum_scatter(block, "bucket", scatter_dimension=0, tiled=True)


def pair_swap(block, parts):
    block = block.reshape(2, -1, block.shape[1])
    return added(swapped(block, "seq", pair_groups(parts))).astype(bf16)


def bucket_swap(block, buckets):
    block = block.reshape(buckets, -1, block.shape[1])
    return added(swapped(block, "bucket")).astype(bf16)


def line_sum(block, parts):
    lines = [[2 * z + c for z in range(parts // 2)] for c in range(2)]
    block = block.reshape(parts // 2, -1, block.shape[1])
    return added(swapped(block, "seq", lines)).astype(bf16)


def gathered(block):
    return lax.all_gather(block, "bucket", axis=0, tiled=True).astype(f32)


def shared_out(block, buckets):
    cols = block.shape[1]
    block = swapped(jnp.broadcast_to(block, (buckets,) + block.shape), "bucket")
    return block.reshape(-1, cols).astype(f32)


def on_device(
    inputs,
    cotangent,
    lengths,
    norm_gains,
    norm_biases,
    in_weight,
    in_bias,
    short_conv,
    long_skip,
    filter_in,
    filter_mid,
    filter_vecs,
    filter_out,
    decay,
    out_weight,
    out_bias,
    up_weight,
    up_bias,
    down_weight,
    down_bias,
):
    seqs, width, dim = inputs.shape
    parts = lax.axis_size("seq")
    index = lax.axis_index("seq")
    chans = dim // parts
    fits = chans % LANES == 0
    blocks = parts if fits else 1
    row = lambda v: v.reshape(1, -1)
    gain1, gain2 = norm_gains[0:1], norm_gains[1:2]
    shift1, shift2 = norm_biases[0:1], norm_biases[1:2]
    skip = row(long_skip)
    tables = transform_tables()

    def to_channels(block):
        if not fits:
            block = jnp.swapaxes(block.reshape(width, parts, chans), 0, 1)
        got = lax.all_to_all(block, "seq", split_axis=0, concat_axis=0, tiled=True)
        got = got.reshape(LEN, chans)
        return got if fits else jnp.pad(got, ((0, 0), (0, LANES - chans)))

    def to_positions(block):
        block = block[:, :chans].reshape(parts, width, chans)
        got = lax.all_to_all(block, "seq", split_axis=0, concat_axis=0, tiled=True)
        return got if fits else jnp.swapaxes(got, 0, 1).reshape(1, width, dim)

    rims = passed_along(inputs[:, width - 2 :, :], "seq", 1)
    rims = jnp.pad(rims, ((0, 0), (14, 0), (0, 0)))
    flag = (index > 0).astype(f32).reshape(1, 1)
    counts = jnp.clip(lengths - index * width, 0, width)

    buckets = lax.axis_size("bucket")

    data, carried = [], []
    shared = ()
    for s in range(seqs):
        got = front(s, inputs, rims, flag, gain1, shift1, in_weight, row(in_bias), short_conv,
                    blocks, shared)
        shared, token = got[:3], got[4]
        carried.append(got[3])
        data.append(to_channels(got[3]))
    normed, proj, mixed = shared

    start = index * chans
    columns = lax.dynamic_slice_in_dim(filter_out, start, chans, 1)
    rates = lax.dynamic_slice_in_dim(decay, start, chans, 0)

    def make_taps(first_w, mid_w, vecs, cols):
        return filter_taps(first_w, mid_w, vecs, cols, rates)

    taps, taps_pull = jax.vjp(make_taps, filter_in, filter_mid, filter_vecs, columns)
    taps_spec = taps_transform(
        taps if fits else jnp.pad(taps, ((0, 0), (0, LANES - chans))), tables, (data[0],)
    )

    specs, convs = [], []
    for s in range(seqs):
        conv, spec, token = long_conv(data[s], taps_spec, tables, None, (token,))
        specs.append(spec)
        convs.append(to_positions(conv))

    mid_sums, grad_convs, grads = [], [], []
    shared = ()
    for s in range(seqs):
        got = middle(
            s, counts[s : s + 1], convs[s], carried[s], mixed, inputs, cotangent, skip, gain2,
            shift2, out_weight, row(out_bias), up_weight, row(up_bias), down_weight,
            row(down_bias), shared, (token,),
        )
        shared, token = got[:9], got[10]
        mid_sums.append(got[10:])
        grad_convs.append(got[9])
        grads.append(to_channels(got[9]))
    output, act, grad_hidden, normed2, gated, grad_down_in, grad_branch, resid, grad_gate = shared

    up, token = weight_grad(normed2, grad_hidden, parts, buckets, (token, grads[0]))
    down, token = weight_grad(act, grad_down_in, parts, buckets, (token,))
    up, token = launched(up, (token, grads[-1]))
    up = pair_sum(up, parts)
    down, token = launched(down, (token,))
    down = pair_sum(down, parts)

    gate_rims = tied(grad_gate.reshape(seqs, width, dim)[:, :2], token)
    gate_rims = passed_along(gate_rims, "seq", -1).astype(f32)
    gate_rims = jnp.pad(gate_rims, ((0, 0), (0, 6), (0, 0)))

    corrs, gbacks = [], []
    for s in range(seqs):
        back, corr, token = long_conv(grads[s], taps_spec, tables, specs[s], (token,))
        if s == 0:
            up, token = launched(up, (token,))
            up = bucket_sum(up)
        corrs.append(corr)
        gbacks.append(to_positions(back))
    grad_first, d_short1, d_bias1, token = gate_grads(
        seqs, grad_gate, proj, gate_rims, short_conv[:, :dim], (token,)
    )
    both, token = two_weight_grads(
        gated, grad_branch, normed, grad_first, parts, buckets, (token,)
    )
    down, token = launched(down, (token, gbacks[0], up))
    down = bucket_sum(down)
    both, token = launched(both, (token,))
    both = pair_sum(both, parts)

    def first_rows(block):
        return jnp.swapaxes(block[:, :2], 0, 1).reshape(2, dim).astype(f32)

    grad_taps, token = taps_back(corrs, tables, (token,))
    d_fin, d_fmid, d_fvecs, d_cols = taps_pull(grad_taps[:, :chans])

    rim_rows = []
    for s in range(seqs):
        grad_carried = first_rows(gbacks[s]) + skip * first_rows(grad_convs[s])
        edge = mixed[s * width : s * width + 2].astype(f32)
        rim_rows.append(
            jnp.concatenate(
                [grad_carried * edge[:, 2 * dim :], grad_carried * edge[:, dim : 2 * dim]], axis=1
            )
        )
    rim = passed_along(tied(jnp.stack(rim_rows), d_fin), "seq", -1)
    rim = jnp.pad(rim, ((0, 0), (0, 6), (0, 0)))
    pair_sums = []
    shared = ()
    both, token = launched(both, (token, d_fin, d_cols, gbacks[-1]))
    both = bucket_sum(both)
    up, token = launched(up, (token,))
    up = line_sum(up, parts)
    hold = ()
    for s in range(seqs):
        got = pair_grads(s, seqs, gbacks[s], grad_convs[s], mixed, proj, rim[s], skip,
                         short_conv[:, dim:], shared, (token,) + hold)
        hold = (up,)
        shared, token = got[:1], got[3]
        pair_sums.append(got[1:3])
    grad_rest = shared[0]
    down = line_sum(down, parts)
    rest, token = weight_grad(normed, grad_rest, parts, buckets, (token, down))
    rest = pair_swap(rest, parts)
    rest = bucket_swap(rest, buckets)
    end_sums = []
    shared = ()
    hold = ()
    for s in range(seqs):
        got = input_grads(s, grad_first, grad_rest, inputs, resid, gain1, in_weight, shared,
                          (token,) + hold)
        shared, token = got[:1], got[3]
        end_sums.append(got[1:3])
        hold = (both,)
    d_up_weight = gathered(up)
    d_down_weight = gathered(down)
    last = line_sum(jnp.concatenate([both, rest], axis=1), parts)
    last = shared_out(last, buckets)
    d_out_weight, d_in_weight = last[:, :dim], last[:, dim:]
    input_grad = shared[0]

    def summed(lists, n):
        total = lists[0][n]
        for other in lists[1:]:
            total = total + other[n]
        return total

    small = [
        jnp.concatenate([summed(end_sums, 0), summed(mid_sums, 0)], axis=0),
        jnp.concatenate([summed(end_sums, 1), summed(mid_sums, 1)], axis=0),
        jnp.concatenate([d_bias1, summed(pair_sums, 1)], axis=1),
        jnp.concatenate([d_short1, summed(pair_sums, 0)], axis=1),
        summed(mid_sums, 5),
        d_fin,
        d_fmid,
        d_fvecs,
        summed(mid_sums, 4),
        summed(mid_sums, 3),
        summed(mid_sums, 2),
    ]
    flat = jnp.concatenate(
        [
            jnp.swapaxes(piece.reshape(piece.shape[0], parts, -1), 0, 1).reshape(parts, -1)
            for piece in small
        ],
        axis=1,
    )
    flat = added(swapped(flat, "seq"))
    flat = jnp.concatenate([flat, d_cols.reshape(-1)])
    flat = added(swapped(jnp.broadcast_to(flat, (buckets,) + flat.shape), "bucket"))
    shares = []
    at = 0
    for shape in [piece.shape for piece in small] + [d_cols.shape]:
        share = shape[1] if len(shares) == len(small) else shape[1] // parts
        shares.append(flat[at : at + shape[0] * share].reshape(shape[0], share))
        at += shape[0] * share
    (d_gains, d_shifts, d_in_bias, d_short, d_skip, d_fin, d_fmid, d_fvecs, d_out_b, d_up_b,
     d_down_b, d_fout) = shares

    return (
        output,
        input_grad,
        d_gains,
        d_shifts,
        d_in_weight,
        d_in_bias.reshape(-1),
        d_short,
        d_skip.reshape(-1),
        d_fin,
        d_fmid,
        d_fvecs,
        d_fout,
        d_out_weight,
        d_out_b.reshape(-1),
        d_up_weight,
        d_up_b.reshape(-1),
        d_down_weight,
        d_down_b.reshape(-1),
    )


def solution(mesh):
    whole = P()
    in_specs = (P("bucket", "seq", None),) * 2 + (P("bucket"),) + (whole,) * 17
    rows, cols, flat = P("seq", None), P(None, "seq"), P("seq")
    out_specs = (
        P("bucket", "seq", None),
        P("bucket", "seq", None),
        cols,
        cols,
        rows,
        flat,
        cols,
        flat,
        cols,
        cols,
        cols,
        cols,
        rows,
        flat,
        rows,
        flat,
        rows,
        flat,
    )
    return jax.shard_map(
        on_device, mesh=mesh, in_specs=in_specs, out_specs=out_specs, check_vma=False
    )
```

profile of v0, /device:TPU:0, one launch (start us, length us, event | category | flops | bytes accessed | tf_op | source)
XLA Modules:
  0.0 804.6 jit_solution(2883101021436998009)
XLA Ops:
  12.5 19.5 %shard_map.367 = (bf16[2048,1024]{1,0:T(8,128)(2,1)}, bf16[2048,3072]{1,0:T(8,128)(2,1)}, bf16[2048,3072]{1,0:T(8,128)(2,1)}, bf16[8,1024,128]{2,1,0:T(8,128)(2,1)}, f32[8,128]{1,0:T(8,128)}) custom-call(bf16[2,1024,1024]{2,1,0:T(8,128)(2,1)} %x_ref.11, bf16[2,16,1024]{2,1,0:T(8,128)(2,1)} %pad.26.rim_ref, f32[1,1]{1,0:T(1,128)} %bitcast.flag_ref, ...), custom_call_target="tpu_custom_call" | custom-call | flops 22000001024 | bytes 1000 | tf_op jit(solution)/shard_map/pallas_call | solution.py:458
  45.5 20.2 %shard_map.368 = (bf16[2048,1024]{1,0:T(8,128)(2,1)}, bf16[2048,3072]{1,0:T(8,128)(2,1)}, bf16[2048,3072]{1,0:T(8,128)(2,1)}, bf16[8,1024,128]{2,1,0:T(8,128)(2,1)}, f32[8,128]{1,0:T(8,128)}) custom-call(bf16[2,1024,1024]{2,1,0:T(8,128)(2,1)} %x_ref.11, ...), custom_call_target="tpu_custom_call", output_to_operand_aliasing={{0}: (8, {}), {1}: (9, {}), {2}: (10, {})} | custom-call | flops 22000001024 | bytes 1000 | tf_op jit(solution)/shard_map/pallas_call | solution.py:458
  65.8 23.2 %all-to-all-done.1 = bf16[8,1024,128]{2,1,0:T(8,128)(2,1)} async-done(((bf16[8,1024,128]{2,1,0:T(8,128)(2,1)}), bf16[8,1024,128]{2,1,0:T(8,128)(2,1)}, u32[]{:S(2)}, u32[]{:S(2)}) %all-to-all-start.1) | async-done | bytes 2097184 | tf_op jit(solution)/shard_map/all_to_all | solution.py:1036
  102.6 26.9 %convolution_multiply_fusion.x_ref = f32[8192,128]{1,0:T(8,128)} fusion(f32[8192]{0:T(1024)S(1)} %iota_convert_fusion, f32[128]{0:T(128)S(1)} %dynamic-slice_negate_fusion, f32[8192,64]{0,1:T(8,128)S(1)} %convolution_add_fusion, f32[64]{0:T(128)S(1)} %get-tuple-element.271, f32[64,1024]{1,0:T(8,128)S(1)} %copy-done, s32[]{:T(128)S(6)} %select_n.14), kind=kOutput, calls=%fused_computation | convolution fusion | flops 807927808 | bytes 6358020 | tf_op jit(solution)/shard_map/jvp()/dot_general | solution.py:44
  138.3 11.6 %shard_map.370 = (bf16[8192,128]{1,0:T(8,128)(2,1)}, bf16[64,256,128]{2,1,0:T(8,128)(2,1)}, f32[8,128]{1,0:T(8,128)}) custom-call(bf16[8192,128]{1,0:T(8,128)(2,1)} %bitcast.7.refs_0_.x_ref, bf16[64,256,128]{2,1,0:T(8,128)(2,1)} %shard_map.369.h_ref, bf16[128,128,128]{2,1,0:T(8,128)(2,1)} %constant.49.clone.ta_ref.refs_0_.refs_1_, ...), custom_call_target="tpu_custom_call" | custom-call | flops 15399999488 | bytes 1000 | tf_op jit(solution)/shard_map/pallas_call | solution.py:243
  167.2 36.9 %all-to-all-done.3.conv_ref = bf16[8,1024,128]{2,1,0:T(8,128)(2,1)S(1)} async-done(((bf16[8,1024,128]{2,1,0:T(8,128)(2,1)}), bf16[8,1024,128]{2,1,0:T(8,128)(2,1)S(1)}, u32[]{:S(2)}, u32[]{:S(2)}) %all-to-all-start.3) | async-done | bytes 2097184 | tf_op jit(solution)/shard_map/all_to_all | solution.py:1042
  209.0 65.5 %shard_map.372 = (bf16[2,1024,1024]{2,1,0:T(8,128)(2,1)}, bf16[2048,4096]{1,0:T(8,128)(2,1)}, bf16[2048,4096]{1,0:T(8,128)(2,1)}, bf16[2048,1024]{1,0:T(8,128)(2...) custom-call(s32[1]{0:T(128)} %get-tuple-element.275.count_ref, ...), custom_call_target="tpu_custom_call" | custom-call | flops 72600002560 | bytes 1000 | tf_op jit(solution)/shard_map/pallas_call | solution.py:594
  280.9 65.8 %shard_map.373 = (bf16[2,1024,1024]{2,1,0:T(8,128)(2,1)}, bf16[2048,4096]{1,0:T(8,128)(2,1)}, bf16[2048,4096]{1,0:T(8,128)(2,1)}, bf16[2048,1024]{1,0:T(8,128)(2...) custom-call(s32[1]{0:T(128)} %get-tuple-element.276.count_ref, ...), custom_call_target="tpu_custom_call", output_to_operand_aliasing={{0}: (15, {}), {1}: (16, {}), {2}: (17, {}), {3}: (18, {}),... | custom-call | flops 72600002560 | bytes 1000 | tf_op jit(solution)/shard_map/pallas_call | solution.py:594
  353.2 22.9 %shard_map.374 = (bf16[2,4,4,32,4096]{4,3,2,1,0:T(8,128)(2,1)}, f32[8,128]{1,0:T(8,128)}) custom-call(bf16[2048,1024]{1,0:T(8,128)(2,1)} %get-tuple-element.140.left, bf16[2048,4096]{1,0:T(8,128)(2,1)} %get-tuple-element.141.right, f32[1,1024]{1,0:T(1,128)} %get-tuple-element.142.refs_0_, bf16[8192,128]{1,0:T(8,128)(2,1)} %bitcast.160), custom_call_target="tpu_custom_call" | custom-call | flops 25300000768 | bytes 1000 | tf_op jit(solution)/shard_map/pallas_call | solution.py:915
  376.1 23.0 %shard_map.375 = (bf16[2,4,4,128,1024]{4,3,2,1,0:T(8,128)(2,1)}, f32[8,128]{1,0:T(8,128)}) custom-call(bf16[2048,4096]{1,0:T(8,128)(2,1)} %get-tuple-element.138.left, bf16[2048,1024]{1,0:T(8,128)(2,1)} %get-tuple-element.139.right, f32[8,128]{1,0:T(8,128)} %get-tuple-element.144.refs_0_), custom_call_target="tpu_custom_call" | custom-call | flops 25300000768 | bytes 1000 | tf_op jit(solution)/shard_map/pallas_call | solution.py:915
  405.0 14.5 %shard_map.378 = (bf16[8192,128]{1,0:T(8,128)(2,1)}, bf16[64,256,128]{2,1,0:T(8,128)(2,1)}, f32[8,128]{1,0:T(8,128)}) custom-call(bf16[8192,128]{1,0:T(8,128)(2,1)} %bitcast.161, bf16[64,256,128]{2,1,0:T(8,128)(2,1)} %shard_map.369.h_ref, bf16[64,256,128]{2,1,0:T(8,128)(2,1)} %get-tuple-element.153.refs_0_, ...), custom_call_target="tpu_custom_call" | custom-call | flops 15399999488 | bytes 1000 | tf_op jit(solution)/shard_map/pallas_call | solution.py:243
  432.0 16.3 %shard_map.380 = (bf16[8192,128]{1,0:T(8,128)(2,1)}, bf16[64,256,128]{2,1,0:T(8,128)(2,1)}, f32[8,128]{1,0:T(8,128)}) custom-call(bf16[8192,128]{1,0:T(8,128)(2,1)} %bitcast.156, bf16[64,256,128]{2,1,0:T(8,128)(2,1)} %shard_map.369.h_ref, bf16[64,256,128]{2,1,0:T(8,128)(2,1)} %get-tuple-element.151.refs_0_, ...), custom_call_target="tpu_custom_call" | custom-call | flops 15399999488 | bytes 1000 | tf_op jit(solution)/shard_map/pallas_call | solution.py:243
  459.1 15.6 %shard_map.382 = (bf16[2,4,4,32,2048]{4,3,2,1,0:T(8,128)(2,1)}, f32[8,128]{1,0:T(8,128)}) custom-call(bf16[2048,1024]{1,0:T(8,128)(2,1)} %get-tuple-element.162.left, bf16[2048,1024]{1,0:T(8,128)(2,1)} %get-tuple-element.163.right, bf16[2048,1024]{1,0:T(8,128)(2,1)} %get-tuple-element.164.left2.left, bf16[2048,1024]{1,0:T(8,128)(2,1)} %get-tuple-element.157.right2.first_ref, ...), custom_call_target="tpu_custom_call" | custom-call | flops 19800000512 | bytes 1000 | tf_op jit(solution)/shard_map/pallas_call | solution.py:874
  480.2 17.5 %reduce-scatter.11.cloned.1.call-done.refs_3_.refs_0_ = bf16[128,4096]{1,0:T(8,128)(2,1)} async-done(((bf16[512,4096]{1,0:T(8,128)(2,1)}), bf16[128,4096]{1,0:T(8,128)(2,1)}) %reduce-scatter.11.cloned.1.call-update) | async-done | bytes 1048592 | tf_op jit(solution)/shard_map/reduce_scatter | solution.py:970
  515.4 15.4 %multiply_reduce_fusion.3 = (f32[64]{0:T(128)}, f32[64]{0:T(128)}, f32[8192,64]{0,1:T(8,128)S(1)}) fusion(f32[64]{0:T(128)S(1)} %copy-done.30, f32[8192,64]{0,1:T(8,128)S(1)} %copy-done.2, f32[64,1024]{1,0:T(8,128)S(1)} %copy-done, s32[]{:T(128)S(6)} %select_n.14, f32[8192,128]{1,0:T(8,128)} %get-tuple-element.172, f32[8192]{0:T(1024)S(1)} %copy-done.18, ...), kind=kOutput, calls=%fused_computation.21 | convolution fusion | flops 810549120 | bytes 8455684 | tf_op jit(solution)/shard_map/transpose(jvp())/dot_general | solution.py:44
  561.9 24.5 %all-to-all-done.8 = bf16[4,32,4096]{2,1,0:T(8,128)(2,1)S(1)} async-done(((bf16[4,32,4096]{2,1,0:T(8,128)(2,1)}), bf16[4,32,4096]{2,1,0:T(8,128)(2,1)S(1)}, u32[]{:S(2)}, u32[]{:S(2)}) %all-to-all-start.8) | async-done | bytes 1048608 | tf_op jit(solution)/shard_map/all_to_all | solution.py:928
  610.6 13.1 %shard_map.388 = (bf16[2048,2048]{1,0:T(8,128)(2,1)}, f32[4,2048]{1,0:T(4,128)}, f32[1,2048]{1,0:T(1,128)}, f32[8,128]{1,0:T(8,128)}) custom-call(bf16[8,1024,128]{2,1,0:T(8,128)(2,1)} %copy-done.8, bf16[8,1024,128]{2,1,0:T(8,128)(2,1)} %get-tuple-element.143.gconv_ref, bf16[2048,3072]{1,0:T(8,128)(2,1)} %get-tuple-element.122.gate_ref.gates_ref, ...), custom_call_target="tpu_custom_call" | custom-call | flops 12099999744 | bytes 1000 | tf_op jit(solution)/shard_map/pallas_call | solution.py:744
  624.6 12.2 %all-to-all-done.9 = bf16[4,128,1024]{2,1,0:T(8,128)(2,1)S(1)} async-done(((bf16[4,128,1024]{2,1,0:T(8,128)(2,1)}), bf16[4,128,1024]{2,1,0:T(8,128)(2,1)S(1)}, u32[]{:S(2)}, u32[]{:S(2)}) %all-to-all-start.9) | async-done | bytes 1048608 | tf_op jit(solution)/shard_map/all_to_all | solution.py:928
  637.6 13.2 %shard_map.389 = (bf16[2048,2048]{1,0:T(8,128)(2,1)}, f32[4,2048]{1,0:T(4,128)}, f32[1,2048]{1,0:T(1,128)}, f32[8,128]{1,0:T(8,128)}) custom-call(bf16[8,1024,128]{2,1,0:T(8,128)(2,1)} %all-to-all-done.6.refs_4_.gback_ref, bf16[8,1024,128]{2,1,0:T(8,128)(2,1)} %get-tuple-element.148.gconv_ref, ...), custom_call_target="tpu_custom_call", output_to_operand_aliasing={{0}: (7, {})} | custom-call | flops 12099999744 | bytes 1000 | tf_op jit(solution)/shard_map/pallas_call | solution.py:744
  650.8 13.3 %shard_map.390 = (bf16[2,4,4,32,2048]{4,3,2,1,0:T(8,128)(2,1)}, f32[8,128]{1,0:T(8,128)}) custom-call(bf16[2048,1024]{1,0:T(8,128)(2,1)} %get-tuple-element.164.left2.left, bf16[2048,2048]{1,0:T(8,128)(2,1)} %get-tuple-element.180.right.rest_ref, f32[8,128]{1,0:T(8,128)} %get-tuple-element.182.refs_0_, bf16[128,1024]{1,0:T(8,128)(2,1)} %fusion.51.refs_1_), custom_call_target="tpu_custom_call" | custom-call | flops 25300000768 | bytes 1000 | tf_op jit(solution)/shard_map/pallas_call | solution.py:915
  680.8 14.5 %shard_map.391 = (f32[2,1024,1024]{2,1,0:T(8,128)}, f32[1,1024]{1,0:T(1,128)}, f32[1,1024]{1,0:T(1,128)}, f32[8,128]{1,0:T(8,128)}) custom-call(bf16[2048,1024]{1,0:T(8,128)(2,1)} %get-tuple-element.157.right2.first_ref, bf16[2048,2048]{1,0:T(8,128)(2,1)} %get-tuple-element.180.right.rest_ref, bf16[2,1024,1024]{2,1,0:T(8,128)(2,1)} %x_ref.11, ...), custom_call_target="tpu_custom_call" | custom-call | flops 15399999488 | bytes 1000 | tf_op jit(solution)/shard_map/pallas_call | solution.py:801
  695.4 12.4 %all-to-all-done.13 = bf16[4,128,2048]{2,1,0:T(8,128)(2,1)} async-done(((bf16[4,128,2048]{2,1,0:T(8,128)(2,1)}), bf16[4,128,2048]{2,1,0:T(8,128)(2,1)}, u32[]{:S(2)}, u32[]{:S(2)}) %all-to-all-start.13) | async-done | bytes 2097184 | tf_op jit(solution)/shard_map/all_to_all | solution.py:928
  712.4 14.6 %shard_map.392 = (f32[2,1024,1024]{2,1,0:T(8,128)}, f32[1,1024]{1,0:T(1,128)}, f32[1,1024]{1,0:T(1,128)}, f32[8,128]{1,0:T(8,128)}) custom-call(bf16[2048,1024]{1,0:T(8,128)(2,1)} %get-tuple-element.157.right2.first_ref, bf16[2048,2048]{1,0:T(8,128)(2,1)} %get-tuple-element.180.right.rest_ref, ...), custom_call_target="tpu_custom_call", output_to_operand_aliasing={{0}: (6, {})} | custom-call | flops 15399999488 | bytes 1000 | tf_op jit(solution)/shard_map/pallas_call | solution.py:801
  753.3 23.7 %all-to-all-done.14 = bf16[4,32,4096]{2,1,0:T(8,128)(2,1)S(1)} async-done(((bf16[4,32,4096]{2,1,0:T(8,128)(2,1)}), bf16[4,32,4096]{2,1,0:T(8,128)(2,1)S(1)}, u32[]{:S(2)}, u32[]{:S(2)}) %all-to-all-start.14) | async-done | bytes 1048608 | tf_op jit(solution)/shard_map/all_to_all | solution.py:928
  (265 shorter events, 251.0 us)
Async XLA Ops:
  32.0 57.0 %all-to-all-start.1 = ((bf16[8,1024,128]{2,1,0:T(8,128)(2,1)}), bf16[8,1024,128]{2,1,0:T(8,128)(2,1)}, u32[]{:S(2)}, u32[]{:S(2)}) async-start(bf16[8,1024,128]{2,1,0:T(8,128)(2,1)} %get-tuple-element.118.carried_ref), calls=%async_computation.1 | async-start | bytes 4194304 | tf_op jit(solution)/shard_map/all_to_all | solution.py:1036
  89.0 60.9 %all-to-all-start = ((bf16[8,1024,128]{2,1,0:T(8,128)(2,1)}), bf16[8,1024,128]{2,1,0:T(8,128)(2,1)}, u32[]{:S(2)}, u32[]{:S(2)}) async-start(bf16[8,1024,128]{2,1,0:T(8,128)(2,1)} %get-tuple-element.117.carried_ref), calls=%async_computation | async-start | bytes 4194304 | tf_op jit(solution)/shard_map/all_to_all | solution.py:1036
  149.9 54.1 %all-to-all-start.3 = ((bf16[8,1024,128]{2,1,0:T(8,128)(2,1)}), bf16[8,1024,128]{2,1,0:T(8,128)(2,1)S(1)}, u32[]{:S(2)}, u32[]{:S(2)}) async-start(bf16[8,1024,128]{2,1,0:T(8,128)(2,1)} %bitcast.164), calls=%async_computation.3 | async-start | bytes 4194304 | tf_op jit(solution)/shard_map/all_to_all | solution.py:1042
  205.4 69.2 %all-to-all-start.2 = ((bf16[8,1024,128]{2,1,0:T(8,128)(2,1)}), bf16[8,1024,128]{2,1,0:T(8,128)(2,1)S(1)}, u32[]{:S(2)}, u32[]{:S(2)}) async-start(bf16[8,1024,128]{2,1,0:T(8,128)(2,1)} %bitcast.163), calls=%async_computation.2 | async-start | bytes 4194304 | tf_op jit(solution)/shard_map/all_to_all | solution.py:1042
  275.9 70.8 %all-to-all-start.4 = ((bf16[8,1024,128]{2,1,0:T(8,128)(2,1)}), bf16[8,1024,128]{2,1,0:T(8,128)(2,1)S(1)}, u32[]{:S(2)}, u32[]{:S(2)}) async-start(bf16[8,1024,128]{2,1,0:T(8,128)(2,1)} %get-tuple-element.143.gconv_ref), calls=%async_computation.4 | async-start | bytes 4194304 | tf_op jit(solution)/shard_map/all_to_all | solution.py:1036
  348.1 54.2 %all-to-all-start.5 = ((bf16[8,1024,128]{2,1,0:T(8,128)(2,1)}), bf16[8,1024,128]{2,1,0:T(8,128)(2,1)S(1)}, u32[]{:S(2)}, u32[]{:S(2)}) async-start(bf16[8,1024,128]{2,1,0:T(8,128)(2,1)} %get-tuple-element.148.gconv_ref), calls=%async_computation.5 | async-start | bytes 4194304 | tf_op jit(solution)/shard_map/all_to_all | solution.py:1036
  353.2 66.8 %reduce-scatter.7.cloned.1.call-start = ((), (), s32[]{:S(2)}) async-start(), calls=%async_computation.22 | async-start | bytes 12582912 | tf_op jit(solution)/shard_map/reduce_scatter | solution.py:964
  404.2 76.0 %reduce-scatter.9.cloned.1.call-start = ((), (), s32[]{:S(2)}) async-start(), calls=%async_computation.23 | async-start | bytes 12582912 | tf_op jit(solution)/shard_map/reduce_scatter | solution.py:964
  404.9 92.8 %reduce-scatter.11.cloned.1.call-start = ((), (), s32[]{:S(2)}) async-start(), calls=%async_computation.24 | async-start | bytes 5242880 | tf_op jit(solution)/shard_map/reduce_scatter | solution.py:970
  425.1 55.0 %all-to-all-start.7 = ((bf16[8,1024,128]{2,1,0:T(8,128)(2,1)}), bf16[8,1024,128]{2,1,0:T(8,128)(2,1)S(1)}, u32[]{:S(2)}, u32[]{:S(2)}) async-start(bf16[8,1024,128]{2,1,0:T(8,128)(2,1)} %bitcast.162), calls=%async_computation.8 | async-start | bytes 4194304 | tf_op jit(solution)/shard_map/all_to_all | solution.py:1042
  431.1 122.8 %reduce-scatter.13.cloned.1.call-start = ((), (), s32[]{:S(2)}) async-start(), calls=%async_computation.25 | async-start | bytes 6291456 | tf_op jit(solution)/shard_map/reduce_scatter | solution.py:964
  498.9 107.4 %reduce-scatter.15.cloned.1.call-start = ((), (), s32[]{:S(2)}) async-start(), calls=%async_computation.26 | async-start | bytes 5242880 | tf_op jit(solution)/shard_map/reduce_scatter | solution.py:970
  499.5 54.4 %all-to-all-start.6 = ((bf16[8,1024,128]{2,1,0:T(8,128)(2,1)}), bf16[8,1024,128]{2,1,0:T(8,128)(2,1)}, u32[]{:S(2)}, u32[]{:S(2)}) async-start(bf16[8,1024,128]{2,1,0:T(8,128)(2,1)} %bitcast.20), calls=%async_computation.7 | async-start | bytes 4194304 | tf_op jit(solution)/shard_map/all_to_all | solution.py:1042
  555.2 31.2 %all-to-all-start.8 = ((bf16[4,32,4096]{2,1,0:T(8,128)(2,1)}), bf16[4,32,4096]{2,1,0:T(8,128)(2,1)S(1)}, u32[]{:S(2)}, u32[]{:S(2)}) async-start(bf16[4,32,4096]{2,1,0:T(8,128)(2,1)} %bitcast.158), calls=%async_computation.12 | async-start | bytes 2097152 | tf_op jit(solution)/shard_map/all_to_all | solution.py:928
  560.4 149.2 %all-gather.5.cloned.1.call-start = ((), (), s32[]{:S(2)}) async-start(), calls=%async_computation.28 | async-start | bytes 1310720 | tf_op jit(solution)/shard_map/all_gather | solution.py:990
  592.8 12.8 %collective-permute-start.2 = (f32[2,2,2048]{2,1,0:T(2,128)}, f32[2,2,2048]{2,1,0:T(2,128)S(1)}, u32[]{:S(2)}, u32[]{:S(2)}) collective-permute-start(f32[2,2,2048]{2,1,0:T(2,128)} %maximum_add_fusion), channel_id=1, source_target_pairs={{1,0},{2,1},{3,2},{4,3},{5,4},{6,5},{7,6},{9,8},{10,9},{11,10},{12... | collective-permute-start | bytes 98312 | tf_op jit(solution)/shard_map/ppermute | solution.py:40
  606.3 30.5 %all-to-all-start.9 = ((bf16[4,128,1024]{2,1,0:T(8,128)(2,1)}), bf16[4,128,1024]{2,1,0:T(8,128)(2,1)S(1)}, u32[]{:S(2)}, u32[]{:S(2)}) async-start(bf16[4,128,1024]{2,1,0:T(8,128)(2,1)} %bitcast.165), calls=%async_computation.14 | async-start | bytes 2097152 | tf_op jit(solution)/shard_map/all_to_all | solution.py:928
  609.8 102.5 %reduce-scatter.17.cloned.1.call-start = ((), (), s32[]{:S(2)}) async-start(), calls=%async_computation.27 | async-start | bytes 2621440 | tf_op jit(solution)/shard_map/reduce_scatter | solution.py:970
  674.8 32.9 %all-to-all-start.13 = ((bf16[4,128,2048]{2,1,0:T(8,128)(2,1)}), bf16[4,128,2048]{2,1,0:T(8,128)(2,1)}, u32[]{:S(2)}, u32[]{:S(2)}) async-start(bf16[4,128,2048]{2,1,0:T(8,128)(2,1)} %bitcast.157), calls=%async_computation.19 | async-start | bytes 4194304 | tf_op jit(solution)/shard_map/all_to_all | solution.py:928
  679.4 53.4 %all-gather.7.cloned.1.call-start = ((), (), s32[]{:S(2)}) async-start(), calls=%async_computation.29 | async-start | bytes 1310720 | tf_op jit(solution)/shard_map/all_gather | solution.py:990
  729.3 10.3 %all-to-all-start.10 = ((f32[8,1,4136]{2,1,0:T(1,128)}), f32[8,1,4136]{2,1,0:T(1,128)S(1)}, u32[]{:S(2)}, u32[]{:S(2)}) async-start(f32[8,1,4136]{2,1,0:T(1,128)} %all_to_all.62), calls=%async_computation.16 | async-start | bytes 270336 | tf_op jit(solution)/shard_map/all_to_all | solution.py:928
  740.5 8.5 %all-to-all-start.11 = ((f32[4,1,12328]{2,1,0:T(1,128)}), f32[4,1,12328]{2,1,0:T(1,128)S(1)}, u32[]{:S(2)}, u32[]{:S(2)}) async-start(f32[4,1,12328]{2,1,0:T(1,128)} %broadcast_in_dim.4), calls=%async_computation.17 | async-start | bytes 397312 | tf_op jit(solution)/shard_map/all_to_all | solution.py:928
  749.0 28.0 %all-to-all-start.14 = ((bf16[4,32,4096]{2,1,0:T(8,128)(2,1)}), bf16[4,32,4096]{2,1,0:T(8,128)(2,1)S(1)}, u32[]{:S(2)}, u32[]{:S(2)}) async-start(bf16[4,32,4096]{2,1,0:T(8,128)(2,1)} %bitcast.64), calls=%async_computation.20 | async-start | bytes 2097152 | tf_op jit(solution)/shard_map/all_to_all | solution.py:928
  778.3 16.6 %all-to-all-start.15 = ((bf16[4,32,4096]{2,1,0:T(8,128)(2,1)}), bf16[4,32,4096]{2,1,0:T(8,128)(2,1)S(1)}, u32[]{:S(2)}, u32[]{:S(2)}) async-start(bf16[4,32,4096]{2,1,0:T(8,128)(2,1)} %broadcast_in_dim.5), calls=%async_computation.21 | async-start | bytes 2097152 | tf_op jit(solution)/shard_map/all_to_all | solution.py:928
  (57 other events, 1043.2 us)
Sparse Core Ops, SparseCore 0:
  404.3 15.6 reduce-scatter.6
  422.4 18.3 reduce-scatter.8
  443.8 53.9 reduce-scatter.10
  500.0 12.0 reduce-scatter.12
  514.9 53.9 reduce-scatter.14
  587.4 24.7 all-gather.4
  615.5 35.2 reduce-scatter.16
  682.7 36.9 all-gather.6
where the time goes:
time: 811 us; the launch traced here: 805 us
  Pallas kernels  390 us (48%)
  waiting for transfers between devices  177 us (22%)
  matrix products  86.3 us (11%)
  starting transfers between devices  75.6 us (9%)
  other arithmetic  25.5 us (3%)
  local copies, waits for them, and re-layouts  24.9 us (3%)
  between operations  17 us (2%)
  blocking collectives  8.48 us (1%)
    pallas_call x2, Pallas kernels, middle(): pl.pallas_call(mid_kernel, grid=(tiles,), in_specs=[pl.BlockSpec(memory_s...  131 us
    all_to_all x7, waiting for transfers between devices, swapped(): lax.all_to_all(block, axis, split_axis=0, concat_axis=0, tiled=True, axis...  88.6 us
    dot_general x8, matrix products, best_dot(): return jnp.dot(left, right, precision=lax.Precision.HIGHEST)  86.3 us
    pallas_call x3, Pallas kernels, weight_grad(): pl.pallas_call(tall_kernel if tall else flat_kernel, grid=(steps,), in_sp...  59.2 us
    pallas_call x4, Pallas kernels, long_conv(): pl.pallas_call(functools.partial(conv_kernel, backward), in_specs=[ANYWHE...  54 us
    all_to_all x4, waiting for transfers between devices, to_positions(): got = lax.all_to_all(block, 'seq', split_axis=0, concat_axis=0, tiled=True)  42.3 us
    pallas_call x2, Pallas kernels, front(): pl.pallas_call(front_kernel, grid=(tiles,), in_specs=[pl.BlockSpec((None,...  39.7 us
    pallas_call x2, Pallas kernels, input_grads(): pl.pallas_call(input_kernel, grid=(tiles,), in_specs=[stacked(dim), stack...  29.1 us
  transfers between devices with their start and end apart: 26, of which 13 were waited for; matrix products, arithmetic and copies ran while one was open for 15% of the time, Pallas kernels for 46%

commit v1 on v0

--- a/solution.py
+++ b/solution.py
@@ -19,6 +19,7 @@
 STEP_F = 8
 ROWS_K = KB + 1
 ROWS_F = 2 * KB + 1
+ROWS_E = 48
 MID_TILE = 256
 MID_BLOCK = 512
 
@@ -40,10 +41,6 @@
     return lax.ppermute(block, axis, route)
 
 
-def best_dot(left, right):
-    return jnp.dot(left, right, precision=lax.Precision.HIGHEST)
-
-
 def dot(left, right):
     return jnp.dot(left, right, preferred_element_type=f32)
 
@@ -52,20 +49,68 @@
     return lax.dot_general(left, right, (((1,), (1,)), ((), ())), preferred_element_type=f32)
 
 
-def positions_embed(length):
-    steps = jnp.arange(length, dtype=jnp.int32)
-    bands = jnp.arange((EMB - 1) // 2, dtype=jnp.int32)
-    angle = 2.0 * math.pi * (steps[:, None] * bands[None, :] % length).astype(f32) / length
-    first = steps[:, None].astype(f32) / (length - 1)
-    return jnp.concatenate([first, jnp.cos(angle), -jnp.sin(angle)], axis=1)
-
-
-def filter_taps(filter_in, filter_mid, filter_vecs, columns, rates):
-    emb = positions_embed(LEN)
-    first = jnp.sin(filter_vecs[1] * (best_dot(emb, filter_in) + filter_vecs[0]))
-    second = jnp.sin(filter_vecs[3] * (best_dot(first, filter_mid) + filter_vecs[2]))
-    steps = jnp.arange(LEN, dtype=jnp.int32).astype(f32)
-    return best_dot(second, columns) * jnp.exp(-rates[None, :] * steps[:, None])
+def positions_table():
+    steps = np.arange(LEN)
+    bands = np.arange((EMB - 1) // 2)
+    angle = 2.0 * np.pi * (bands[:, None] * steps[None, :] % LEN) / LEN
+    first = steps[None, :] / (LEN - 1)
+    table = np.concatenate([first, np.cos(angle), -np.sin(angle)], axis=0)
+    return jnp.asarray(np.pad(table, ((0, ROWS_E - EMB), (0, 0))).astype(np.float32))
+
+
+def halves(block):
+    high = block.astype(bf16)
+    return high, (block - high.astype(f32)).astype(bf16)
+
+
+def exact(left, right, contract):
+    high, low = halves(left)
+    left = jnp.concatenate([high, high, low], axis=contract[0][0])
+    high, low = halves(right)
+    right = jnp.concatenate([high, low, high], axis=contract[1][0])
+    return lax.dot_general(left, right, (contract, ((), ())), preferred_element_type=f32)
+
+
+def sine_series(r):
+    square = r * r
+    poly = -1.0 / 39916800.0
+    for term in (1.0 / 362880.0, -1.0 / 5040.0, 1.0 / 120.0, -1.0 / 6.0):
+        poly = poly * square + term
+    return r + r * square * poly
+
+
+def without_turns(x, n):
+    return x - n * 3.140625 - n * 9.67502593994140625e-4 - n * 1.509957990978376432e-7
+
+
+def sign_of(n):
+    return 1.0 - 2.0 * (n.astype(jnp.int32) & 1).astype(f32)
+
+
+def sine(x):
+    n = jnp.floor(x * (1.0 / math.pi) + 0.5)
+    return sign_of(n) * sine_series(without_turns(x, n))
+
+
+def cosine(x):
+    n = jnp.floor(x * (1.0 / math.pi))
+    return -sign_of(n) * sine_series(without_turns(x, n + 0.5))
+
+
+CHUNK = 1024
+
+
+def filter_layers(emb, w_in, w_mid, vecs):
+    bias1, freq1, bias2, freq2 = (vecs[:, n : n + 1] for n in range(4))
+    at1 = exact(w_in, emb, ((1,), (0,))) + bias1
+    first = sine(freq1 * at1)
+    at2 = exact(w_mid, first, ((1,), (0,))) + bias2
+    return at1, first, at2
+
+
+def window(first, rates):
+    steps = (first + lax.broadcasted_iota(jnp.int32, (KB, LANES), 0)).astype(f32)
+    return jnp.exp(-rates * steps)
 
 
 def transform_tables():
@@ -144,7 +189,7 @@
 def packed(src, dst):
     for m in range(HALF):
         rows = src[m * ROWS_K : m * ROWS_K + KB] * (1.0 / LEN)
-        dst[m * KB : (m + 1) * KB] = rows.astype(dst.dtype)
+        dst[m * KB : (m + 1) * KB] = rows.astype(bf16)
 
 
 def row_pair(at):
@@ -264,14 +309,21 @@
     )(rows, taps_spec, *extra, onward, back, inner, inner_back, *after)
 
 
-def taps_kernel(x_ref, ta_ref, tb, *refs):
-    h_ref, x, ta, xs, mid, h, sems = refs[-7:]
-    x_in = fetch(x_ref, x, sems, 0, 2)
-    ta_in = fetch(ta_ref, ta, sems, 2, PIECES)
-    half = HALF // 2
-    for n in range(2):
-        x_in[n].wait()
-        spaced(x, xs, n * half, half)
+def taps_kernel(emb, w_in, w_mid, vecs, cols, rates, ta_ref, tb, *refs):
+    h_ref, ta, xs, mid, h, sems = refs[-6:]
+    ta_in = fetch(ta_ref, ta, sems, 0, PIECES)
+
+    def chunk(c, carry):
+        part = pl.ds(pl.multiple_of(c * CHUNK, CHUNK), CHUNK)
+        _, _, at2 = filter_layers(emb[:, part], w_in[...], w_mid[...], vecs)
+        second = sine(vecs[:, 3:4] * at2)
+        taps = exact(second, cols[...], ((0,), (0,)))
+        for n in range(CHUNK // KB):
+            m = c * (CHUNK // KB) + n
+            xs[pl.ds(m * ROWS_K, KB), :] = taps[n * KB : (n + 1) * KB] * window(m * KB, rates[...])
+        return carry
+
+    lax.fori_loop(0, LEN // CHUNK, chunk, 0)
     for n in range(PIECES):
         ta_in[n].wait()
         outer_stage(n * KB // PIECES, KB // PIECES, False, xs, ta, mid)
@@ -288,37 +340,36 @@
     for n in range(PIECES):
         looped(rows // 2, STEP_F, lambda at, n=n: body(n * rows // 2 + at))
         part = pl.ds(n * rows, rows)
-        copy = pltpu.make_async_copy(h.at[part], h_ref.at[part], sems.at[2 + PIECES + n])
+        copy = pltpu.make_async_copy(h.at[part], h_ref.at[part], sems.at[PIECES + n])
         copy.start()
         leaving.append(copy)
     for copy in leaving:
         copy.wait()
 
 
-def taps_transform(taps, tables, after):
+def taps_transform(network, tables, after):
     onward, _, inner, _ = tables
     return pl.pallas_call(
         taps_kernel,
-        in_specs=[ANYWHERE, ANYWHERE, IN_VMEM] + [ANYWHERE] * len(after),
+        in_specs=[IN_VMEM] * 6 + [ANYWHERE, IN_VMEM] + [ANYWHERE] * len(after),
         out_specs=ANYWHERE,
         out_shape=jax.ShapeDtypeStruct(SPECTRUM, bf16),
         scratch_shapes=[
-            pltpu.VMEM((LEN, LANES), f32),
             pltpu.VMEM(onward.shape, bf16),
             pltpu.VMEM((HALF * ROWS_K, LANES), f32),
             pltpu.VMEM((HALF * ROWS_F, LANES), f32),
             pltpu.VMEM(SPECTRUM, bf16),
-            pltpu.SemaphoreType.DMA((2 + 2 * PIECES,)),
+            pltpu.SemaphoreType.DMA((2 * PIECES,)),
         ],
         compiler_params=pltpu.CompilerParams(vmem_limit_bytes=60 * MIB),
         cost_estimate=lasting(15),
-    )(taps, onward, inner, *after)
+    )(*network, onward, inner, *after)
 
 
 def taps_back_kernel(count, *refs):
     specs = refs[:count]
-    tai_ref, tbi = refs[count : count + 2]
-    y_ref, token, tai, mid, ys, held, sems = refs[-7:]
+    tai_ref, tbi, emb, w_in, w_mid, vecs, cols, rates = refs[count : count + 8]
+    d_in, d_mid, d_vecs, d_cols, token, tai, mid, ys, held, sems = refs[-10:]
     token[...] = jnp.zeros_like(token)
     tai_in = fetch(tai_ref, tai, sems, 0, 1)
     arrivals = [
@@ -344,17 +395,48 @@
         looped(rows // 2, STEP_F, lambda at, n=n: body(n * rows // 2 + at))
     tai_in[0].wait()
     outer_back(0, KB, mid, tai, ys)
-    packed(ys, y_ref)
-
-
-def taps_back(specs, tables, after):
+    for ref in (d_in, d_mid, d_vecs, d_cols):
+        ref[...] = jnp.zeros_like(ref)
+
+    def chunk(c, carry):
+        part = pl.ds(pl.multiple_of(c * CHUNK, CHUNK), CHUNK)
+        at1, first, at2 = filter_layers(emb[:, part], w_in[...], w_mid[...], vecs)
+        freq1, freq2 = vecs[:, 1:2], vecs[:, 3:4]
+        second = sine(freq2 * at2)
+        rows = []
+        for n in range(CHUNK // KB):
+            m = c * (CHUNK // KB) + n
+            rows.append(ys[pl.ds(m * ROWS_K, KB), :] * (window(m * KB, rates[...]) * (1.0 / LEN)))
+        grad = jnp.concatenate(rows, axis=0)
+        d_cols[...] += exact(second, grad, ((1,), (0,)))
+        turn2 = exact(cols[...], grad, ((1,), (1,))) * cosine(freq2 * at2)
+        inner2 = turn2 * freq2
+        d_mid[...] += exact(first, inner2, ((1,), (1,)))
+        turn1 = exact(w_mid[...], inner2, ((0,), (0,))) * cosine(freq1 * at1)
+        inner1 = turn1 * freq1
+        d_in[...] += exact(emb[:, part], inner1, ((1,), (1,)))
+        for n, terms in enumerate((inner1, turn1 * at1, inner2, turn2 * at2)):
+            d_vecs[:, n : n + 1] += jnp.sum(terms, axis=1, keepdims=True)
+        return carry
+
+    lax.fori_loop(0, LEN // CHUNK, chunk, 0)
+
+
+def taps_back(specs, tables, network, after):
     _, back, _, inner_back = tables
     count = len(specs)
+    hidden = network[2].shape[0]
     return pl.pallas_call(
         functools.partial(taps_back_kernel, count),
-        in_specs=[ANYWHERE] * (count + 1) + [IN_VMEM] + [ANYWHERE] * len(after),
-        out_specs=[IN_VMEM, IN_VMEM],
-        out_shape=[jax.ShapeDtypeStruct((LEN, LANES), f32), TOKEN],
+        in_specs=[ANYWHERE] * (count + 1) + [IN_VMEM] * 7 + [ANYWHERE] * len(after),
+        out_specs=[IN_VMEM] * 5,
+        out_shape=[
+            jax.ShapeDtypeStruct((ROWS_E, hidden), f32),
+            jax.ShapeDtypeStruct((hidden, hidden), f32),
+            jax.ShapeDtypeStruct((hidden, 4), f32),
+            jax.ShapeDtypeStruct((hidden, LANES), f32),
+            TOKEN,
+        ],
         scratch_shapes=[
             pltpu.VMEM(back.shape, bf16),
             pltpu.VMEM((HALF * ROWS_F, LANES), f32),
@@ -363,8 +445,8 @@
             pltpu.SemaphoreType.DMA((1 + count * PIECES,)),
         ],
         compiler_params=pltpu.CompilerParams(vmem_limit_bytes=60 * MIB),
-        cost_estimate=lasting(15),
-    )(*specs, back, inner_back, *after)
+        cost_estimate=lasting(20),
+    )(*specs, back, inner_back, *network, *after)
 
 
 def normalized(rows):
@@ -447,7 +529,7 @@
         spread_out(carried_ref, first, (parts[1] * parts[2]).astype(bf16))
 
 
-def front(s, inputs, rims, flag, gain, shift, weight, bias, short, blocks, shared):
+def front(s, inputs, rims, flag, gain, shift, weight, bias, short, blocks, shared, after):
     seqs, width, dim = inputs.shape
     tile = min(256, width)
     tiles = width // tile
@@ -468,7 +550,7 @@
             once((1, wide)),
             once((4, wide)),
         ]
-        + [ANYWHERE] * len(shared),
+        + [ANYWHERE] * (len(shared) + len(after)),
         out_specs=[
             stacked(dim),
             stacked(wide),
@@ -487,7 +569,7 @@
         scratch_shapes=[pltpu.VMEM((8, wide), f32)],
         compiler_params=pltpu.CompilerParams(vmem_limit_bytes=60 * MIB),
         cost_estimate=lasting(20),
-    )(*operands, *shared)
+    )(*operands, *shared, *after)
 
 
 def gelu_and_slope(hidden):
@@ -970,6 +1052,16 @@
     return lax.psum_scatter(block, "bucket", scatter_dimension=0, tiled=True)
 
 
+def line_groups(parts):
+    return [[2 * z + c for z in range(parts // 2)] for c in range(2)]
+
+
+def line_scatter(block, parts):
+    return lax.psum_scatter(
+        block, "seq", scatter_dimension=0, tiled=True, axis_index_groups=line_groups(parts)
+    )
+
+
 def pair_swap(block, parts):
     block = block.reshape(2, -1, block.shape[1])
     return added(swapped(block, "seq", pair_groups(parts))).astype(bf16)
@@ -981,13 +1073,8 @@
 
 
 def line_sum(block, parts):
-    lines = [[2 * z + c for z in range(parts // 2)] for c in range(2)]
     block = block.reshape(parts // 2, -1, block.shape[1])
-    return added(swapped(block, "seq", lines)).astype(bf16)
-
-
-def gathered(block):
-    return lax.all_gather(block, "bucket", axis=0, tiled=True).astype(f32)
+    return added(swapped(block, "seq", line_groups(parts))).astype(bf16)
 
 
 def shared_out(block, buckets):
@@ -1049,27 +1136,30 @@
 
     buckets = lax.axis_size("bucket")
 
+    start = index * chans
+    columns = lax.dynamic_slice_in_dim(filter_out, start, chans, 1)
+    rates = lax.dynamic_slice_in_dim(decay, start, chans, 0)
+
+    network = (
+        positions_table(),
+        jnp.pad(filter_in.T, ((0, 0), (0, ROWS_E - EMB))),
+        filter_mid.T,
+        filter_vecs.T,
+        jnp.pad(columns, ((0, 0), (0, LANES - chans))) if not fits else columns,
+        row(jnp.pad(rates, (0, LANES - chans)) if not fits else rates),
+    )
     data, carried = [], []
-    shared = ()
+    shared = after = ()
     for s in range(seqs):
         got = front(s, inputs, rims, flag, gain1, shift1, in_weight, row(in_bias), short_conv,
-                    blocks, shared)
+                    blocks, shared, after)
         shared, token = got[:3], got[4]
         carried.append(got[3])
         data.append(to_channels(got[3]))
+        if s == 0:
+            taps_spec = taps_transform(network, tables, (token,))
+            after = (taps_spec,)
     normed, proj, mixed = shared
-
-    start = index * chans
-    columns = lax.dynamic_slice_in_dim(filter_out, start, chans, 1)
-    rates = lax.dynamic_slice_in_dim(decay, start, chans, 0)
-
-    def make_taps(first_w, mid_w, vecs, cols):
-        return filter_taps(first_w, mid_w, vecs, cols, rates)
-
-    taps, taps_pull = jax.vjp(make_taps, filter_in, filter_mid, filter_vecs, columns)
-    taps_spec = taps_transform(
-        taps if fits else jnp.pad(taps, ((0, 0), (0, LANES - chans))), tables, (data[0],)
-    )
 
     specs, convs = [], []
     for s in range(seqs):
@@ -1091,41 +1181,44 @@
         grads.append(to_channels(got[9]))
     output, act, grad_hidden, normed2, gated, grad_down_in, grad_branch, resid, grad_gate = shared
 
-    up, token = weight_grad(normed2, grad_hidden, parts, buckets, (token, grads[0]))
+    corrs, gbacks = [], []
+    back, corr, token = long_conv(grads[0], taps_spec, tables, specs[0], (token,))
+    corrs.append(corr)
+    up, token = weight_grad(normed2, grad_hidden, parts, buckets, (token,))
     down, token = weight_grad(act, grad_down_in, parts, buckets, (token,))
     up, token = launched(up, (token, grads[-1]))
     up = pair_sum(up, parts)
     down, token = launched(down, (token,))
     down = pair_sum(down, parts)
+    gbacks.append(to_positions(back))
 
     gate_rims = tied(grad_gate.reshape(seqs, width, dim)[:, :2], token)
     gate_rims = passed_along(gate_rims, "seq", -1).astype(f32)
     gate_rims = jnp.pad(gate_rims, ((0, 0), (0, 6), (0, 0)))
 
-    corrs, gbacks = [], []
-    for s in range(seqs):
+    for s in range(1, seqs):
         back, corr, token = long_conv(grads[s], taps_spec, tables, specs[s], (token,))
-        if s == 0:
-            up, token = launched(up, (token,))
-            up = bucket_sum(up)
         corrs.append(corr)
         gbacks.append(to_positions(back))
+    up, token = launched(up, (token,))
+    up = bucket_sum(up)
     grad_first, d_short1, d_bias1, token = gate_grads(
         seqs, grad_gate, proj, gate_rims, short_conv[:, :dim], (token,)
     )
     both, token = two_weight_grads(
         gated, grad_branch, normed, grad_first, parts, buckets, (token,)
     )
-    down, token = launched(down, (token, gbacks[0], up))
+    both, token = launched(both, (token, gbacks[0]))
+    both = pair_sum(both, parts)
+    down, token = launched(down, (token,))
     down = bucket_sum(down)
-    both, token = launched(both, (token,))
-    both = pair_sum(both, parts)
 
     def first_rows(block):
         return jnp.swapaxes(block[:, :2], 0, 1).reshape(2, dim).astype(f32)
 
-    grad_taps, token = taps_back(corrs, tables, (token,))
-    d_fin, d_fmid, d_fvecs, d_cols = taps_pull(grad_taps[:, :chans])
+    d_fin, d_fmid, d_fvecs, d_cols, token = taps_back(corrs, tables, network, (token,))
+    gbacks[-1], token = launched(gbacks[-1], (token,))
+    d_fin, d_fvecs, d_cols = d_fin[:EMB], d_fvecs.T, d_cols[:, :chans]
 
     rim_rows = []
     for s in range(seqs):
@@ -1136,37 +1229,42 @@
                 [grad_carried * edge[:, 2 * dim :], grad_carried * edge[:, dim : 2 * dim]], axis=1
             )
         )
-    rim = passed_along(tied(jnp.stack(rim_rows), d_fin), "seq", -1)
+    rim = passed_along(jnp.stack(rim_rows), "seq", -1)
     rim = jnp.pad(rim, ((0, 0), (0, 6), (0, 0)))
     pair_sums = []
     shared = ()
-    both, token = launched(both, (token, d_fin, d_cols, gbacks[-1]))
-    both = bucket_sum(both)
+    both, token = launched(both, (token,))
+    both = bucket_swap(both, buckets)
     up, token = launched(up, (token,))
-    up = line_sum(up, parts)
-    hold = ()
+    up = line_scatter(up, parts)
+    shared = ()
+    pair_sums = []
     for s in range(seqs):
         got = pair_grads(s, seqs, gbacks[s], grad_convs[s], mixed, proj, rim[s], skip,
-                         short_conv[:, dim:], shared, (token,) + hold)
-        hold = (up,)
+                         short_conv[:, dim:], shared, (token,))
         shared, token = got[:1], got[3]
         pair_sums.append(got[1:3])
     grad_rest = shared[0]
-    down = line_sum(down, parts)
-    rest, token = weight_grad(normed, grad_rest, parts, buckets, (token, down))
-    rest = pair_swap(rest, parts)
-    rest = bucket_swap(rest, buckets)
+    rest, token = weight_grad(normed, grad_rest, parts, buckets, (token, both))
+    rest_half = pair_swap(rest, parts)
+    rest = bucket_swap(rest_half, buckets)
     end_sums = []
     shared = ()
-    hold = ()
+    hold = (rest_half,)
     for s in range(seqs):
         got = input_grads(s, grad_first, grad_rest, inputs, resid, gain1, in_weight, shared,
                           (token,) + hold)
         shared, token = got[:1], got[3]
+        hold = ()
+        if s == 0:
+            down, token = launched(down, (token,))
+            down = line_scatter(down, parts)
         end_sums.append(got[1:3])
-        hold = (both,)
-    d_up_weight = gathered(up)
-    d_down_weight = gathered(down)
+    pair = jnp.concatenate([up.reshape(-1, dim), down], axis=0)
+    pair = lax.all_gather(pair, "bucket", axis=0, tiled=True).astype(f32)
+    pair = pair.reshape(buckets, 2, -1, dim)
+    d_up_weight = pair[:, 0].reshape(dim // parts, -1)
+    d_down_weight = pair[:, 1].reshape(-1, dim)
     last = line_sum(jnp.concatenate([both, rest], axis=1), parts)
     last = shared_out(last, buckets)
     d_out_weight, d_in_weight = last[:, :dim], last[:, dim:]
@@ -1198,7 +1296,7 @@
         ],
         axis=1,
     )
-    flat = added(swapped(flat, "seq"))
+    flat = added(swapped(tied(flat, rest), "seq"))
     flat = jnp.concatenate([flat, d_cols.reshape(-1)])
     flat = added(swapped(jnp.broadcast_to(flat, (buckets,) + flat.shape), "bucket"))
     shares = []

time: 811 us -> 738 us (0.910)
  matrix products: 86.3 us -> 0 us
  Pallas kernels: 390 us -> 411 us
  local copies, waits for them, and re-layouts: 24.9 us -> 39.7 us
  waiting for transfers between devices: 177 us -> 165 us
  starting transfers between devices: 75.6 us -> 66.8 us
    dot_general x8 -> x0, matrix products: 86.3 us -> none  [best_dot(): return jnp.dot(left, right, precision=lax.Precision.HIGHEST)]
    all_to_all x7 -> x6, waiting for transfers between devices: 88.6 us -> 44.4 us  [swapped(): lax.all_to_all(block, axis, split_axis=0, concat_axis=0, tiled=True, axis...]
    all_to_all x4, waiting for transfers between devices: 26.4 us -> 50 us  [to_channels(): got = lax.all_to_all(block, 'seq', split_axis=0, concat_axis=0, tiled=True)]
    all_to_all x4, waiting for transfers between devices: 42.3 us -> 63.8 us  [to_positions(): got = lax.all_to_all(block, 'seq', split_axis=0, concat_axis=0, tiled=True)]
    pallas_call x1, Pallas kernels: 11.2 us -> 25.8 us  [taps_back(): pl.pallas_call(functools.partial(taps_back_kernel, count), in_specs=[ANYW...]
    reduce_scatter x3 -> x2, waiting for transfers between devices: 17.5 us -> 3.35 us  [bucket_sum(): return lax.psum_scatter(block, 'bucket', scatter_dimension=0, tiled=True)]
    all_to_all x7 -> x6, starting transfers between devices: 27.2 us -> 22.8 us  [swapped(): lax.all_to_all(block, axis, split_axis=0, concat_axis=0, tiled=True, axis...]
  transfers between devices with their start and end apart: 26 -> 25, of which waited for: 13 -> 13; matrix products, arithmetic and copies ran while one was open for 15% -> 6% of each run, Pallas kernels for 46% -> 53%
where the time goes in v1:
time: 738 us; the launch traced here: 732 us
  Pallas kernels  411 us (56%)
  waiting for transfers between devices  165 us (22%)
  starting transfers between devices  66.8 us (9%)
  local copies, waits for them, and re-layouts  39.7 us (5%)
  other arithmetic  21.3 us (3%)
  between operations  16.6 us (2%)
  blocking collectives  11.2 us (2%)
    pallas_call x2, Pallas kernels, middle(): pl.pallas_call(mid_kernel, grid=(tiles,), in_specs=[pl.BlockSpec(memory_s...  131 us
    all_to_all x4, waiting for transfers between devices, to_positions(): got = lax.all_to_all(block, 'seq', split_axis=0, concat_axis=0, tiled=True)  63.8 us
    pallas_call x3, Pallas kernels, weight_grad(): pl.pallas_call(tall_kernel if tall else flat_kernel, grid=(steps,), in_sp...  59.2 us
    pallas_call x4, Pallas kernels, long_conv(): pl.pallas_call(functools.partial(conv_kernel, backward), in_specs=[ANYWHE...  52.4 us
    all_to_all x4, waiting for transfers between devices, to_channels(): got = lax.all_to_all(block, 'seq', split_axis=0, concat_axis=0, tiled=True)  50 us
    all_to_all x6, waiting for transfers between devices, swapped(): lax.all_to_all(block, axis, split_axis=0, concat_axis=0, tiled=True, axis...  44.4 us
    pallas_call x2, Pallas kernels, front(): pl.pallas_call(front_kernel, grid=(tiles,), in_specs=[pl.BlockSpec((None,...  39 us
    pallas_call x2, Pallas kernels, input_grads(): pl.pallas_call(input_kernel, grid=(tiles,), in_specs=[stacked(dim), stack...  29.3 us
  transfers between devices with their start and end apart: 25, of which 13 were waited for; matrix products, arithmetic and copies ran while one was open for 6% of the time, Pallas kernels for 53%

profile of v1, /device:TPU:0, one launch (start us, length us, event | category | flops | bytes accessed | tf_op | source)
XLA Modules:
  0.0 732.0 jit_solution(267179394557109795)
XLA Ops:
  17.3 19.5 %shard_map.376 = (bf16[2048,1024]{1,0:T(8,128)(2,1)}, bf16[2048,3072]{1,0:T(8,128)(2,1)}, bf16[2048,3072]{1,0:T(8,128)(2,1)}, bf16[8,1024,128]{2,1,0:T(8,128)(2,1)}, f32[8,128]{1,0:T(8,128)}) custom-call(bf16[2,1024,1024]{2,1,0:T(8,128)(2,1)} %x_ref.11, bf16[2,16,1024]{2,1,0:T(8,128)(2,1)} %pad.18.rim_ref, f32[1,1]{1,0:T(1,128)} %bitcast.flag_ref, ...), custom_call_target="tpu_custom_call" | custom-call | flops 22000001024 | bytes 1000 | tf_op jit(solution)/shard_map/pallas_call | solution.py:540
  44.4 15.6 %shard_map.377.refs_3_.h_ref = bf16[64,256,128]{2,1,0:T(8,128)(2,1)} custom-call(f32[48,8192]{1,0:T(8,128)} %constant.35.clone.emb.refs_4_, f32[64,48]{1,0:T(8,128)} %pad.19.w_in.refs_5_, f32[64,64]{1,0:T(8,128)} %bitcast.163, f32[64,4]{1,0:T(8,128)} %bitcast.165, f32[64,128]{1,0:T(8,128)} %constant_dynamic-slice_fusion.cols.refs_8_, ...), custom_call_target="tpu_custom_call" | custom-call | flops 16499999744 | bytes 1000 | tf_op jit(solution)/shard_map/pallas_call | solution.py:352
  60.1 19.5 %shard_map.378 = (bf16[2048,1024]{1,0:T(8,128)(2,1)}, bf16[2048,3072]{1,0:T(8,128)(2,1)}, bf16[2048,3072]{1,0:T(8,128)(2,1)}, bf16[8,1024,128]{2,1,0:T(8,128)(2,1)}, f32[8,128]{1,0:T(8,128)}) custom-call(bf16[2,1024,1024]{2,1,0:T(8,128)(2,1)} %x_ref.11, ...), custom_call_target="tpu_custom_call", output_to_operand_aliasing={{0}: (8, {}), {1}: (9, {}), {2}: (10, {})} | custom-call | flops 22000001024 | bytes 1000 | tf_op jit(solution)/shard_map/pallas_call | solution.py:540
  79.6 12.6 %all-to-all-done.1 = bf16[8,1024,128]{2,1,0:T(8,128)(2,1)S(1)} async-done(((bf16[8,1024,128]{2,1,0:T(8,128)(2,1)}), bf16[8,1024,128]{2,1,0:T(8,128)(2,1)S(1)}, u32[]{:S(2)}, u32[]{:S(2)}) %all-to-all-start.1) | async-done | bytes 2097184 | tf_op jit(solution)/shard_map/all_to_all | solution.py:1123
  96.8 11.6 %shard_map.379 = (bf16[8192,128]{1,0:T(8,128)(2,1)}, bf16[64,256,128]{2,1,0:T(8,128)(2,1)}, f32[8,128]{1,0:T(8,128)}) custom-call(bf16[8192,128]{1,0:T(8,128)(2,1)} %bitcast.150, bf16[64,256,128]{2,1,0:T(8,128)(2,1)} %shard_map.377.refs_3_.h_ref, bf16[128,128,128]{2,1,0:T(8,128)(2,1)} %constant.31.clone.ta_ref.refs_0_.refs_1_, ...), custom_call_target="tpu_custom_call" | custom-call | flops 15399999488 | bytes 1000 | tf_op jit(solution)/shard_map/pallas_call | solution.py:288
  108.4 37.4 %all-to-all-done = bf16[8,1024,128]{2,1,0:T(8,128)(2,1)} async-done(((bf16[8,1024,128]{2,1,0:T(8,128)(2,1)}), bf16[8,1024,128]{2,1,0:T(8,128)(2,1)}, u32[]{:S(2)}, u32[]{:S(2)}) %all-to-all-start) | async-done | bytes 2097184 | tf_op jit(solution)/shard_map/all_to_all | solution.py:1123
  150.1 11.6 %shard_map.380 = (bf16[8192,128]{1,0:T(8,128)(2,1)}, bf16[64,256,128]{2,1,0:T(8,128)(2,1)}, f32[8,128]{1,0:T(8,128)}) custom-call(bf16[8192,128]{1,0:T(8,128)(2,1)} %bitcast.6.x_ref, bf16[64,256,128]{2,1,0:T(8,128)(2,1)} %shard_map.377.refs_3_.h_ref, bf16[128,128,128]{2,1,0:T(8,128)(2,1)} %constant.31.clone.ta_ref.refs_0_.refs_1_, ...), custom_call_target="tpu_custom_call" | custom-call | flops 15399999488 | bytes 1000 | tf_op jit(solution)/shard_map/pallas_call | solution.py:288
  161.6 36.8 %all-to-all-done.3.conv_ref = bf16[8,1024,128]{2,1,0:T(8,128)(2,1)S(1)} async-done(((bf16[8,1024,128]{2,1,0:T(8,128)(2,1)}), bf16[8,1024,128]{2,1,0:T(8,128)(2,1)S(1)}, u32[]{:S(2)}, u32[]{:S(2)}) %all-to-all-start.3) | async-done | bytes 2097184 | tf_op jit(solution)/shard_map/all_to_all | solution.py:1129
  203.5 65.6 %shard_map.381 = (bf16[2,1024,1024]{2,1,0:T(8,128)(2,1)}, bf16[2048,4096]{1,0:T(8,128)(2,1)}, bf16[2048,4096]{1,0:T(8,128)(2,1)}, bf16[2048,1024]{1,0:T(8,128)(2...) custom-call(s32[1]{0:T(128)} %get-tuple-element.285.count_ref, ...), custom_call_target="tpu_custom_call" | custom-call | flops 72600002560 | bytes 1000 | tf_op jit(solution)/shard_map/pallas_call | solution.py:676
  274.2 65.6 %shard_map.382 = (bf16[2,1024,1024]{2,1,0:T(8,128)(2,1)}, bf16[2048,4096]{1,0:T(8,128)(2,1)}, bf16[2048,4096]{1,0:T(8,128)(2,1)}, bf16[2048,1024]{1,0:T(8,128)(2...) custom-call(s32[1]{0:T(128)} %get-tuple-element.286.count_ref, ...), custom_call_target="tpu_custom_call", output_to_operand_aliasing={{0}: (15, {}), {1}: (16, {}), {2}: (17, {}), {3}: (18, {}),... | custom-call | flops 72600002560 | bytes 1000 | tf_op jit(solution)/shard_map/pallas_call | solution.py:676
  345.0 13.9 %shard_map.383 = (bf16[8192,128]{1,0:T(8,128)(2,1)}, bf16[64,256,128]{2,1,0:T(8,128)(2,1)}, f32[8,128]{1,0:T(8,128)}) custom-call(bf16[8192,128]{1,0:T(8,128)(2,1)} %bitcast.15.x_ref, bf16[64,256,128]{2,1,0:T(8,128)(2,1)} %shard_map.377.refs_3_.h_ref, bf16[64,256,128]{2,1,0:T(8,128)(2,1)} %get-tuple-element.152.refs_0_, ...), custom_call_target="tpu_custom_call" | custom-call | flops 15399999488 | bytes 1000 | tf_op jit(solution)/shard_map/pallas_call | solution.py:288
  358.9 22.9 %shard_map.384 = (bf16[2,4,4,32,4096]{4,3,2,1,0:T(8,128)(2,1)}, f32[8,128]{1,0:T(8,128)}) custom-call(bf16[2048,1024]{1,0:T(8,128)(2,1)} %get-tuple-element.149.left, bf16[2048,4096]{1,0:T(8,128)(2,1)} %get-tuple-element.150.right, f32[8,128]{1,0:T(8,128)} %get-tuple-element.154.refs_0_), custom_call_target="tpu_custom_call" | custom-call | flops 25300000768 | bytes 1000 | tf_op jit(solution)/shard_map/pallas_call | solution.py:997
  381.8 23.0 %shard_map.385 = (bf16[2,4,4,128,1024]{4,3,2,1,0:T(8,128)(2,1)}, f32[8,128]{1,0:T(8,128)}) custom-call(bf16[2048,4096]{1,0:T(8,128)(2,1)} %get-tuple-element.147.left, bf16[2048,1024]{1,0:T(8,128)(2,1)} %get-tuple-element.148.right, f32[8,128]{1,0:T(8,128)} %get-tuple-element.155.refs_0_), custom_call_target="tpu_custom_call" | custom-call | flops 25300000768 | bytes 1000 | tf_op jit(solution)/shard_map/pallas_call | solution.py:997
  419.1 15.3 %shard_map.388 = (bf16[8192,128]{1,0:T(8,128)(2,1)}, bf16[64,256,128]{2,1,0:T(8,128)(2,1)}, f32[8,128]{1,0:T(8,128)}) custom-call(bf16[8192,128]{1,0:T(8,128)(2,1)} %bitcast.142, bf16[64,256,128]{2,1,0:T(8,128)(2,1)} %shard_map.377.refs_3_.h_ref, bf16[64,256,128]{2,1,0:T(8,128)(2,1)} %get-tuple-element.163.refs_0_, ...), custom_call_target="tpu_custom_call" | custom-call | flops 15399999488 | bytes 1000 | tf_op jit(solution)/shard_map/pallas_call | solution.py:288
  435.7 11.3 %shard_map.390 = (bf16[2048,1024]{1,0:T(8,128)(2,1)}, f32[4,1024]{1,0:T(4,128)}, f32[1,1024]{1,0:T(1,128)}, f32[8,128]{1,0:T(8,128)}) custom-call(bf16[2048,1024]{1,0:T(8,128)(2,1)} %get-tuple-element.145.ggo_ref, bf16[2048,3072]{1,0:T(8,128)(2,1)} %get-tuple-element.146.proj_ref, f32[2,8,1024]{2,1,0:T(8,128)} %pad_convert_fusion.rim_ref, ...), custom_call_target="tpu_custom_call" | custom-call | flops 7699999744 | bytes 1000 | tf_op jit(solution)/shard_map/pallas_call | solution.py:768
  447.0 15.3 %shard_map.391 = (bf16[2,4,4,32,2048]{4,3,2,1,0:T(8,128)(2,1)}, f32[8,128]{1,0:T(8,128)}) custom-call(bf16[2048,1024]{1,0:T(8,128)(2,1)} %get-tuple-element.171.left, bf16[2048,1024]{1,0:T(8,128)(2,1)} %get-tuple-element.172.right, bf16[2048,1024]{1,0:T(8,128)(2,1)} %get-tuple-element.173.left2.left, bf16[2048,1024]{1,0:T(8,128)(2,1)} %get-tuple-element.166.right2.first_ref, ...), custom_call_target="tpu_custom_call" | custom-call | flops 19800000512 | bytes 1000 | tf_op jit(solution)/shard_map/pallas_call | solution.py:956
  476.2 25.8 %shard_map.394 = (f32[48,64]{1,0:T(8,128)}, f32[64,64]{1,0:T(8,128)}, f32[64,4]{1,0:T(8,128)}, f32[64,128]{1,0:T(8,128)}, f32[8,128]{1,0:T(8,128)}) custom-call(bf16[64,256,128]{2,1,0:T(8,128)(2,1)} %get-tuple-element.168.refs_0_, bf16[64,256,128]{2,1,0:T(8,128)(2,1)} %get-tuple-element.169.refs_1_, bf16[128,64,128]{2,1,0:T(8,128)(2,1)} %constant.32.clone.refs_1_.refs_2_, ...), custom_call_target="tpu_custom_call" | custom-call | flops 22000001024 | bytes 1000 | tf_op jit(solution)/shard_map/pallas_call | solution.py:429
  502.1 21.6 %all-to-all-done.6.refs_0_ = bf16[8,1024,128]{2,1,0:T(8,128)(2,1)S(1)} async-done(((bf16[8,1024,128]{2,1,0:T(8,128)(2,1)}), bf16[8,1024,128]{2,1,0:T(8,128)(2,1)S(1)}, u32[]{:S(2)}, u32[]{:S(2)}) %all-to-all-start.6) | async-done | bytes 2097184 | tf_op jit(solution)/shard_map/all_to_all | solution.py:1129
  538.5 13.6 %shard_map.398 = (bf16[2048,2048]{1,0:T(8,128)(2,1)}, f32[4,2048]{1,0:T(4,128)}, f32[1,2048]{1,0:T(1,128)}, f32[8,128]{1,0:T(8,128)}) custom-call(bf16[8,1024,128]{2,1,0:T(8,128)(2,1)} %copy-done.3, bf16[8,1024,128]{2,1,0:T(8,128)(2,1)} %get-tuple-element.151.gconv_ref, bf16[2048,3072]{1,0:T(8,128)(2,1)} %get-tuple-element.131.gate_ref.gates_ref, ...), custom_call_target="tpu_custom_call" | custom-call | flops 12099999744 | bytes 1000 | tf_op jit(solution)/shard_map/pallas_call | solution.py:826
  552.1 13.3 %shard_map.399 = (bf16[2048,2048]{1,0:T(8,128)(2,1)}, f32[4,2048]{1,0:T(4,128)}, f32[1,2048]{1,0:T(1,128)}, f32[8,128]{1,0:T(8,128)}) custom-call(bf16[8,1024,128]{2,1,0:T(8,128)(2,1)} %get-tuple-element.181.gback_ref, bf16[8,1024,128]{2,1,0:T(8,128)(2,1)} %get-tuple-element.159.gconv_ref, ...), custom_call_target="tpu_custom_call", output_to_operand_aliasing={{0}: (7, {})} | custom-call | flops 12099999744 | bytes 1000 | tf_op jit(solution)/shard_map/pallas_call | solution.py:826
  570.8 13.4 %shard_map.400 = (bf16[2,4,4,32,2048]{4,3,2,1,0:T(8,128)(2,1)}, f32[8,128]{1,0:T(8,128)}) custom-call(bf16[2048,1024]{1,0:T(8,128)(2,1)} %get-tuple-element.173.left2.left, bf16[2048,2048]{1,0:T(8,128)(2,1)} %get-tuple-element.189.right.rest_ref, f32[8,128]{1,0:T(8,128)} %get-tuple-element.191.refs_0_, bf16[128,2048]{1,0:T(8,128)(2,1)} %fusion.14.refs_1_), custom_call_target="tpu_custom_call" | custom-call | flops 25300000768 | bytes 1000 | tf_op jit(solution)/shard_map/pallas_call | solution.py:997
  608.8 14.7 %shard_map.401 = (f32[2,1024,1024]{2,1,0:T(8,128)}, f32[1,1024]{1,0:T(1,128)}, f32[1,1024]{1,0:T(1,128)}, f32[8,128]{1,0:T(8,128)}) custom-call(bf16[2048,1024]{1,0:T(8,128)(2,1)} %get-tuple-element.166.right2.first_ref, bf16[2048,2048]{1,0:T(8,128)(2,1)} %get-tuple-element.189.right.rest_ref, bf16[2,1024,1024]{2,1,0:T(8,128)(2,1)} %x_ref.11, ...), custom_call_target="tpu_custom_call" | custom-call | flops 15399999488 | bytes 1000 | tf_op jit(solution)/shard_map/pallas_call | solution.py:883
  624.1 14.6 %shard_map.403 = (f32[2,1024,1024]{2,1,0:T(8,128)}, f32[1,1024]{1,0:T(1,128)}, f32[1,1024]{1,0:T(1,128)}, f32[8,128]{1,0:T(8,128)}) custom-call(bf16[2048,1024]{1,0:T(8,128)(2,1)} %get-tuple-element.166.right2.first_ref, bf16[2048,2048]{1,0:T(8,128)(2,1)} %get-tuple-element.189.right.rest_ref, ...), custom_call_target="tpu_custom_call", output_to_operand_aliasing={{0}: (6, {})} | custom-call | flops 15399999488 | bytes 1000 | tf_op jit(solution)/shard_map/pallas_call | solution.py:883
  674.6 24.8 %all-to-all-done.13 = bf16[4,32,4096]{2,1,0:T(8,128)(2,1)S(1)} async-done(((bf16[4,32,4096]{2,1,0:T(8,128)(2,1)}), bf16[4,32,4096]{2,1,0:T(8,128)(2,1)S(1)}, u32[]{:S(2)}, u32[]{:S(2)}) %all-to-all-start.13) | async-done | bytes 1048608 | tf_op jit(solution)/shard_map/all_to_all | solution.py:1010
  (219 shorter events, 176.2 us)
Async XLA Ops:
  8.0 8.7 %collective-permute-start = (bf16[2,2,1024]{2,1,0:T(2,128)(2,1)S(1)}, bf16[2,2,1024]{2,1,0:T(2,128)(2,1)S(1)}, u32[]{:S(2)}, u32[]{:S(2)}) collective-permute-start(bf16[2,2,1024]{2,1,0:T(2,128)(2,1)S(1)} %slice.246), channel_id=1, source_target_pairs={{0,1},{1,2},{2,3},{3,4},{4,5},{5,6},{6,7},{8,9},{9,10},{10,11},{11... | collective-permute-start | bytes 24584 | tf_op jit(solution)/shard_map/ppermute | solution.py:41
  36.8 55.4 %all-to-all-start.1 = ((bf16[8,1024,128]{2,1,0:T(8,128)(2,1)}), bf16[8,1024,128]{2,1,0:T(8,128)(2,1)S(1)}, u32[]{:S(2)}, u32[]{:S(2)}) async-start(bf16[8,1024,128]{2,1,0:T(8,128)(2,1)} %get-tuple-element.127.carried_ref), calls=%async_computation.1 | async-start | bytes 4194304 | tf_op jit(solution)/shard_map/all_to_all | solution.py:1123
  92.2 53.6 %all-to-all-start = ((bf16[8,1024,128]{2,1,0:T(8,128)(2,1)}), bf16[8,1024,128]{2,1,0:T(8,128)(2,1)}, u32[]{:S(2)}, u32[]{:S(2)}) async-start(bf16[8,1024,128]{2,1,0:T(8,128)(2,1)} %get-tuple-element.126.carried_ref), calls=%async_computation | async-start | bytes 4194304 | tf_op jit(solution)/shard_map/all_to_all | solution.py:1123
  145.8 52.6 %all-to-all-start.3 = ((bf16[8,1024,128]{2,1,0:T(8,128)(2,1)}), bf16[8,1024,128]{2,1,0:T(8,128)(2,1)S(1)}, u32[]{:S(2)}, u32[]{:S(2)}) async-start(bf16[8,1024,128]{2,1,0:T(8,128)(2,1)} %bitcast.151), calls=%async_computation.3 | async-start | bytes 4194304 | tf_op jit(solution)/shard_map/all_to_all | solution.py:1129
  199.9 69.2 %all-to-all-start.2 = ((bf16[8,1024,128]{2,1,0:T(8,128)(2,1)}), bf16[8,1024,128]{2,1,0:T(8,128)(2,1)S(1)}, u32[]{:S(2)}, u32[]{:S(2)}) async-start(bf16[8,1024,128]{2,1,0:T(8,128)(2,1)} %bitcast.149), calls=%async_computation.2 | async-start | bytes 4194304 | tf_op jit(solution)/shard_map/all_to_all | solution.py:1129
  269.2 70.7 %all-to-all-start.4 = ((bf16[8,1024,128]{2,1,0:T(8,128)(2,1)}), bf16[8,1024,128]{2,1,0:T(8,128)(2,1)}, u32[]{:S(2)}, u32[]{:S(2)}) async-start(bf16[8,1024,128]{2,1,0:T(8,128)(2,1)} %get-tuple-element.151.gconv_ref), calls=%async_computation.4 | async-start | bytes 4194304 | tf_op jit(solution)/shard_map/all_to_all | solution.py:1123
  339.8 64.9 %all-to-all-start.5 = ((bf16[8,1024,128]{2,1,0:T(8,128)(2,1)}), bf16[8,1024,128]{2,1,0:T(8,128)(2,1)S(1)}, u32[]{:S(2)}, u32[]{:S(2)}) async-start(bf16[8,1024,128]{2,1,0:T(8,128)(2,1)} %get-tuple-element.159.gconv_ref), calls=%async_computation.5 | async-start | bytes 4194304 | tf_op jit(solution)/shard_map/all_to_all | solution.py:1123
  345.0 90.1 %reduce-scatter.8.cloned.1.call-start = ((), (), s32[]{:S(2)}) async-start(), calls=%async_computation.22 | async-start | bytes 12582912 | tf_op jit(solution)/shard_map/reduce_scatter | solution.py:1046
  406.7 63.6 %reduce-scatter.10.cloned.1.call-start = ((), (), s32[]{:S(2)}) async-start(), calls=%async_computation.23 | async-start | bytes 12582912 | tf_op jit(solution)/shard_map/reduce_scatter | solution.py:1046
  411.3 23.1 %collective-permute-start.1 = (bf16[2,2,1024]{2,1,0:T(2,128)(2,1)S(1)}, bf16[2,2,1024]{2,1,0:T(2,128)(2,1)S(1)}, u32[]{:S(2)}, u32[]{:S(2)}) collective-permute-start(bf16[2,2,1024]{2,1,0:T(2,128)(2,1)S(1)} %slice_add_fusion.10), channel_id=1, source_target_pairs={{1,0},{2,1},{3,2},{4,3},{5,4},{6,5},{7,6},{9,8},{10,9},{11,10},{12... | collective-permute-start | bytes 24584 | tf_op jit(solution)/shard_map/ppermute | solution.py:41
  412.6 55.1 %all-to-all-start.7 = ((bf16[8,1024,128]{2,1,0:T(8,128)(2,1)}), bf16[8,1024,128]{2,1,0:T(8,128)(2,1)S(1)}, u32[]{:S(2)}, u32[]{:S(2)}) async-start(bf16[8,1024,128]{2,1,0:T(8,128)(2,1)} %bitcast.148), calls=%async_computation.9 | async-start | bytes 4194304 | tf_op jit(solution)/shard_map/all_to_all | solution.py:1129
  418.6 111.6 %reduce-scatter.14.cloned.1.call-start = ((), (), s32[]{:S(2)}) async-start(), calls=%async_computation.25 | async-start | bytes 6291456 | tf_op jit(solution)/shard_map/reduce_scatter | solution.py:1046
  469.6 68.3 %reduce-scatter.12.cloned.1.call-start = ((), (), s32[]{:S(2)}) async-start(), calls=%async_computation.24 | async-start | bytes 5242880 | tf_op jit(solution)/shard_map/reduce_scatter | solution.py:1052
  470.2 153.3 %reduce-scatter.16.cloned.1.call-start = ((), (), s32[]{:S(2)}) async-start(), calls=%async_computation.26 | async-start | bytes 5242880 | tf_op jit(solution)/shard_map/reduce_scatter | solution.py:1052
  470.9 52.8 %all-to-all-start.6 = ((bf16[8,1024,128]{2,1,0:T(8,128)(2,1)}), bf16[8,1024,128]{2,1,0:T(8,128)(2,1)S(1)}, u32[]{:S(2)}, u32[]{:S(2)}) async-start(bf16[8,1024,128]{2,1,0:T(8,128)(2,1)} %bitcast.147), calls=%async_computation.7 | async-start | bytes 4194304 | tf_op jit(solution)/shard_map/all_to_all | solution.py:1129
  530.8 38.9 %all-to-all-start.8 = ((bf16[4,128,2048]{2,1,0:T(8,128)(2,1)}), bf16[4,128,2048]{2,1,0:T(8,128)(2,1)S(1)}, u32[]{:S(2)}, u32[]{:S(2)}) async-start(bf16[4,128,2048]{2,1,0:T(8,128)(2,1)} %bitcast.146), calls=%async_computation.12 | async-start | bytes 4194304 | tf_op jit(solution)/shard_map/all_to_all | solution.py:1010
  534.5 106.1 %reduce-scatter.18.cloned.1.call-start = ((), (), s32[]{:S(2)}) async-start(), calls=%async_computation.27 | async-start | bytes 1310720 | tf_op jit(solution)/shard_map/reduce_scatter | solution.py:1060
  599.6 42.2 %all-to-all-start.10 = ((bf16[4,128,2048]{2,1,0:T(8,128)(2,1)}), bf16[4,128,2048]{2,1,0:T(8,128)(2,1)}, u32[]{:S(2)}, u32[]{:S(2)}) async-start(bf16[4,128,2048]{2,1,0:T(8,128)(2,1)} %bitcast.143), calls=%async_computation.15 | async-start | bytes 4194304 | tf_op jit(solution)/shard_map/all_to_all | solution.py:1010
  604.1 64.2 %reduce-scatter.20.cloned.1.call-start = ((), (), s32[]{:S(2)}) async-start(), calls=%async_computation.28 | async-start | bytes 1310720 | tf_op jit(solution)/shard_map/reduce_scatter | solution.py:1060
  645.7 14.4 %all-to-all-start.11 = ((f32[8,1,4136]{2,1,0:T(1,128)}), f32[8,1,4136]{2,1,0:T(1,128)S(1)}, u32[]{:S(2)}, u32[]{:S(2)}) async-start(f32[8,1,4136]{2,1,0:T(1,128)} %copy.94), calls=%async_computation.16 | async-start | bytes 270336 | tf_op jit(solution)/shard_map/all_to_all | solution.py:1010
  661.0 9.3 %all-to-all-start.12 = ((f32[4,1,12328]{2,1,0:T(1,128)}), f32[4,1,12328]{2,1,0:T(1,128)S(1)}, u32[]{:S(2)}, u32[]{:S(2)}) async-start(f32[4,1,12328]{2,1,0:T(1,128)} %broadcast_in_dim.6), calls=%async_computation.17 | async-start | bytes 397312 | tf_op jit(solution)/shard_map/all_to_all | solution.py:1010
  665.1 54.5 %all-gather.2.cloned.1.call-start = ((), (), s32[]{:S(2)}) async-start(), calls=%async_computation.29 | async-start | bytes 2621440 | tf_op jit(solution)/shard_map/all_gather | solution.py:1264
  670.3 29.1 %all-to-all-start.13 = ((bf16[4,32,4096]{2,1,0:T(8,128)(2,1)}), bf16[4,32,4096]{2,1,0:T(8,128)(2,1)S(1)}, u32[]{:S(2)}, u32[]{:S(2)}) async-start(bf16[4,32,4096]{2,1,0:T(8,128)(2,1)} %pad_maximum_fusion), calls=%async_computation.18 | async-start | bytes 2097152 | tf_op jit(solution)/shard_map/all_to_all | solution.py:1010
  700.6 16.6 %all-to-all-start.14 = ((bf16[4,32,4096]{2,1,0:T(8,128)(2,1)}), bf16[4,32,4096]{2,1,0:T(8,128)(2,1)S(1)}, u32[]{:S(2)}, u32[]{:S(2)}) async-start(bf16[4,32,4096]{2,1,0:T(8,128)(2,1)} %broadcast_in_dim.7), calls=%async_computation.19 | async-start | bytes 2097152 | tf_op jit(solution)/shard_map/all_to_all | solution.py:1010
  (35 other events, 617.0 us)
Sparse Core Ops, SparseCore 0:
  406.8 18.6 reduce-scatter.7
  427.9 17.9 reduce-scatter.9
  469.8 10.9 reduce-scatter.13
  483.9 53.9 reduce-scatter.11
  540.7 62.1 reduce-scatter.15
  605.2 27.1 reduce-scatter.17
  640.3 27.9 reduce-scatter.19
  670.9 33.9 all-gather.1
